TPU v7x, 512 devices: a whole 4x4x16 slice. The times are simulated.
512 devices in a mesh: rep: 16 (over z), head: 32 (over x, y, core).
Axes of the slice: x: 4, y: 4, z: 16, core: 2. Of those that a mesh axis runs over, the one named last changes fastest.
Arguments:
- layer_input: bfloat16 [8192, 8192], P('rep', 'head'), may hold values from -6 to 6
- proj_weight: bfloat16 [8192, 8192], P('rep', 'head'), may hold values from -0.0625 to 0.0625
- step_weight: bfloat16 [8192, 128], P('rep', 'head'), may hold values from -0.0625 to 0.0625
- step_bias: float32 [128], P('head'), may hold values from -4 to 0.5
- decay_log: float32 [128], P('head'), may hold values from -7 to -1
- conv_weight: float32 [4, 8192], P(None, 'head'), may hold values from -3 to 3
- conv_bias: float32 [8192], P('head'), may hold values from -2 to 2
- skip_gain: float32 [128], P('head'), may hold values from 0.5 to 1.5
- group_inputs: bfloat16 [8192, 2048], P('rep', 'head'), may hold values from -1.5 to 1.5
- cached_state: float32 [16, 128, 64, 256], P('rep', 'head'), may hold values from -1.5 to 1.5
- cached_tail: float32 [16, 3, 8192], P('rep', None, 'head'), may hold values from -6 to 6
- owner_map: int32 [16], replicated, may hold values from 0 to 15, each once
- request_state: int32 [16], replicated, may hold values from 0 to 16, as said below
- shared_id: int32 [1], replicated, may hold values from 0 to 15
Outputs:
- ssm_output: bfloat16 [8192, 8192], P('rep', 'head')
- final_state: float32 [16, 128, 64, 256], P('rep', 'head')
- final_tail: float32 [16, 3, 8192], P('rep', None, 'head')
Inputs may be any that keep to these rules, and one draw needn't show every extreme that they name: `request_state`: A value below 16 is a state id; the value 16 means the shared prompt, whose id is shared_id; some request always names it. `owner_map`: each state id has its own cache row.
All inputs are finite; a program needn't handle non-finite values.
Results may differ from a plain program's by a relative error of at most 0.015.
Values may be sent and summed in bfloat16 or wider, within the bound.
A program may use at most 128 MiB of HBM per device.

v0:
```python
import jax
import jax.numpy as jnp
from jax import lax
from jax.sharding import PartitionSpec as P

HEADS = 128
P_SIZE = 64
N = 256
G = 4
KERNEL = 4


def on_device(
    layer_input,
    proj_weight,
    step_weight,
    step_bias,
    decay_log,
    conv_weight,
    conv_bias,
    skip_gain,
    group_inputs,
    cached_state,
    cached_tail,
    owner_map,
    request_state,
    shared_id,
):
    rep_index = lax.axis_index("rep")
    head_index = lax.axis_index("head")
    local_heads = step_bias.shape[0]
    channels = conv_bias.shape[0]
    new_rows = layer_input.shape[0]
    state_count = owner_map.shape[0]
    state_ids = jnp.where(request_state < state_count, request_state, shared_id[0])
    state_rows = owner_map[state_ids]
    row_mine = lax.dynamic_index_in_dim(state_rows, rep_index, 0, keepdims=False)
    needed = state_rows == rep_index
    send_state = jnp.where(needed[:, None, None, None], cached_state, 0.0)
    send_tail = jnp.where(needed[:, None, None], cached_tail, 0.0)
    got_state, got_tail = (
        lax.all_to_all(send_state, "rep", split_axis=0, concat_axis=0, tiled=True),
        lax.all_to_all(send_tail, "rep", split_axis=0, concat_axis=0, tiled=True),
    )
    prior_state = lax.dynamic_index_in_dim(got_state, row_mine, 0, keepdims=False)
    prior_tail = lax.dynamic_index_in_dim(got_tail, row_mine, 0, keepdims=False)
    whole, columns = (
        lax.all_gather(layer_input, "head", axis=1, tiled=True),
        lax.all_gather(group_inputs, "head", axis=1, tiled=True),
    )
    global_heads = head_index * local_heads + jnp.arange(local_heads, dtype=jnp.int32)
    head_group = global_heads // (HEADS // G)
    selector = (head_group[:, None] == jnp.arange(G, dtype=jnp.int32)[None, :]).astype(jnp.bfloat16)
    grouped = columns.reshape(new_rows, G, 2, N)
    picked = jnp.einsum(
        "tgkn,hg->thkn", grouped, selector, preferred_element_type=jnp.float32
    ).astype(jnp.bfloat16)
    in_vec = picked[:, :, 0, :]
    out_vec = picked[:, :, 1, :]
    scores = jnp.einsum("thn,shn->hts", out_vec, in_vec, preferred_element_type=jnp.float32)
    joined_weight = jnp.concatenate([proj_weight, step_weight], axis=1)
    joined_raw = jnp.dot(
        whole,
        lax.all_gather(joined_weight, "rep", axis=0, tiled=True),
        preferred_element_type=jnp.float32,
    )
    proj_raw = joined_raw[:, :channels]
    step_raw = joined_raw[:, channels:]
    projected = proj_raw.astype(jnp.bfloat16)
    step_size = jax.nn.softplus(step_raw + step_bias)
    extended = jnp.concatenate([prior_tail, projected.astype(jnp.float32)], axis=0)
    final_tail = extended[new_rows:]
    conv_sum = conv_bias + conv_weight[0] * extended[0:new_rows]
    for offset in range(1, KERNEL):
        conv_sum = conv_sum + conv_weight[offset] * extended[offset : offset + new_rows]
    conv_out = jax.nn.silu(conv_sum).astype(jnp.bfloat16)
    decay_sum = jnp.cumsum(-jnp.exp(decay_log) * step_size, axis=0)
    lower = jnp.tril(jnp.ones((new_rows, new_rows), dtype=bool))
    differ = decay_sum.T[:, :, None] - decay_sum.T[:, None, :]
    decays = jnp.where(lower[None], jnp.exp(jnp.where(lower[None], differ, 0.0)), 0.0)
    mixing = (scores * decays * step_size.T[:, None, :]).astype(jnp.bfloat16)
    heads_x = conv_out.reshape(new_rows, local_heads, P_SIZE)
    inner = jnp.einsum("hts,shp->thp", mixing, heads_x, preferred_element_type=jnp.float32)
    carried = jnp.einsum(
        "thn,hpn->thp", out_vec.astype(jnp.float32), prior_state, precision=lax.Precision.HIGHEST
    )
    carried = carried * jnp.exp(decay_sum)[:, :, None]
    output = inner + carried + skip_gain[None, :, None] * heads_x.astype(jnp.float32)
    output = output.reshape(new_rows, channels).astype(jnp.bfloat16)
    last = decay_sum[new_rows - 1]
    weights = jnp.exp(last[None, :] - decay_sum) * step_size
    weighted = (heads_x.astype(jnp.float32) * weights[:, :, None]).astype(jnp.bfloat16)
    final_state = jnp.exp(last)[:, None, None] * prior_state + jnp.einsum(
        "thp,thn->hpn", weighted, in_vec, preferred_element_type=jnp.float32
    )
    return (output, final_state[None], final_tail[None])


def solution(mesh):
    return jax.shard_map(
        on_device,
        mesh=mesh,
        in_specs=(
            P("rep", "head"),
            P("rep", "head"),
            P("rep", "head"),
            P("head"),
            P("head"),
            P(None, "head"),
            P("head"),
            P("head"),
            P("rep", "head"),
            P("rep", "head", None, None),
            P("rep", None, "head"),
            P(),
            P(),
            P(),
        ),
        out_specs=(P("rep", "head"), P("rep", "head", None, None), P("rep", None, "head")),
        check_vma=False,
    )
```

profile of v0, /device:TPU:6, one launch (start us, length us, event | category | flops | bytes accessed | tf_op | source)
XLA Modules:
  0.0 395.2 jit_solution(6549845652574865282)
XLA Ops:
  7.2 0.0 copy-start
  7.2 0.0 all-gather.8.cloned.1.call-start
  7.2 0.7 all-gather.8.cloned.1.call-update
  7.9 0.0 all-gather.4.cloned.1.call-start
  8.0 0.9 copy.31
  8.8 1.8 pad_maximum_fusion.1
  10.6 0.0 all-gather.4.cloned.1.call-update
  10.6 0.0 all-gather.6.cloned.1.call-start
  10.7 0.7 all-gather.6.cloned.1.call-update
  11.4 0.7 copy.60
  12.7 0.7 compare_select_fusion.1
  13.4 0.0 copy-done
  13.4 0.7 gather_fusion
  14.1 0.7 broadcast_select_fusion.1
  14.8 15.2 %all-to-all-start = ((f32[16,3,256]{2,1,0:T(4,128)}), f32[16,3,256]{2,1,0:T(4,128)S(1)}, u32[]{:S(2)}, u32[]{:S(2)}) async-start(f32[16,3,256]{2,1,0:T(4,128)} %broadcast_select_fusion.1), calls=%async_computation | async-start | bytes 131072 | tf_op jit(solution)/shard_map/all_to_all | solution.py:43
  30.0 3.5 broadcast_select_fusion
  33.5 0.0 copy-start.5
  33.5 0.0 copy-start.1
  33.5 9.2 %all-to-all-done = f32[16,3,256]{2,1,0:T(4,128)S(1)} async-done(((f32[16,3,256]{2,1,0:T(4,128)}), f32[16,3,256]{2,1,0:T(4,128)S(1)}, u32[]{:S(2)}, u32[]{:S(2)}) %all-to-all-start) | async-done | bytes 49184 | tf_op jit(solution)/shard_map/all_to_all | solution.py:43
  42.7 4.6 %all-to-all-start.1 = ((f32[16,4,64,256]{3,2,1,0:T(8,128)}), f32[16,4,64,256]{3,2,1,0:T(8,128)}, u32[]{:S(2)}, u32[]{:S(2)}) async-start(f32[16,4,64,256]{3,2,1,0:T(8,128)} %broadcast_select_fusion), calls=%async_computation.1 | async-start | bytes 8388608 | tf_op jit(solution)/shard_map/all_to_all | solution.py:42
  47.3 0.6 dynamic_slice.12
  49.8 0.1 iota_compare_fusion
  49.9 0.0 copy-done.5
  49.9 0.0 copy-done.1
  50.0 0.1 copy.30
  50.1 24.2 %all-gather.8.cloned.1.call-done = bf16[512,2048]{0,1:T(8,128)(2,1)} async-done(((bf16[512,64]{0,1:T(8,128)(2,1)}), bf16[512,2048]{0,1:T(8,128)(2,1)}) %all-gather.8.cloned.1.call-update) | async-done | bytes 2097168 | tf_op jit(solution)/shard_map/all_gather | solution.py:49
  74.3 3.4 copy.32
  77.7 1.3 convert_bitcast_fusion
  79.0 0.7 slice_bitcast_fusion.1
  79.8 0.0 copy-start.2
  79.8 0.0 copy-start.3
  79.8 215.1 %all-gather.4.cloned.1.call-done = bf16[8192,260]{1,0:T(8,128)(2,1)} async-done(((bf16[512,260]{1,0:T(8,128)(2,1)}), bf16[8192,260]{1,0:T(8,128)(2,1)}) %all-gather.4.cloned.1.call-update) | async-done | bytes 4259856 | tf_op jit(solution)/shard_map/all_gather | solution.py:64
  294.9 74.4 %all-gather.6.cloned.1.call-done = bf16[512,8192]{1,0:T(8,128)(2,1)} async-done(((bf16[512,256]{1,0:T(8,128)(2,1)}), bf16[512,8192]{1,0:T(8,128)(2,1)}) %all-gather.6.cloned.1.call-update) | async-done | bytes 8388624 | tf_op jit(solution)/shard_map/all_gather | solution.py:48
  369.3 8.7 %convolution_bitcast_fusion = f32[512,260]{0,1:T(8,128)S(1)} fusion(bf16[8192,260]{1,0:T(8,128)(2,1)} %all-gather.4.cloned.1.call-done, bf16[512,8192]{1,0:T(8,128)(2,1)} %all-gather.6.cloned.1.call-done), kind=kOutput, calls=%fused_computation.5 | convolution fusion | flops 2181038080 | bytes 13180928 | tf_op jit(solution)/shard_map/dot_general | solution.py:62
  378.0 0.0 copy-done.2
  378.0 0.1 multiply_bitcast_fusion
  378.1 1.2 reduce-window.6
  379.3 0.2 slice_reduce_fusion
  379.5 0.2 reduce-window.9
  379.7 0.1 add_bitcast_fusion
  379.8 0.2 slice_reduce_fusion.1
  380.0 0.1 exponential_multiply_fusion
  380.1 0.1 slice_bitcast_fusion.2
  380.2 0.0 copy-done.3
  380.2 0.8 multiply_convert_fusion.1
  381.0 0.0 copy-start.4
  381.0 2.2 fusion.1
  383.2 0.0 all-to-all-done.1
  383.2 0.0 copy-done.4
  383.2 2.0 fusion.5
  385.3 0.8 copy.37
  386.1 0.7 copy.38
  386.8 1.9 fusion.6
  (10 shorter events, 0.1 us)
Async XLA Ops:
  7.2 6.2 %copy-start = (s32[16]{0:T(128)S(1)}, s32[16]{0:T(128)}, u32[]{:S(2)}) copy-start(s32[16]{0:T(128)} %param.25) | copy-start | bytes 196
  7.2 67.1 %all-gather.8.cloned.1.call-start = ((), (), s32[]{:S(2)}) async-start(), calls=%async_computation.4 | async-start | bytes 2162688 | tf_op jit(solution)/shard_map/all_gather | solution.py:49
  7.9 286.9 %all-gather.4.cloned.1.call-start = ((), (), s32[]{:S(2)}) async-start(), calls=%async_computation.2 | async-start | bytes 6684672 | tf_op jit(solution)/shard_map/all_gather | solution.py:64
  10.6 358.7 %all-gather.6.cloned.1.call-start = ((), (), s32[]{:S(2)}) async-start(), calls=%async_computation.3 | async-start | bytes 8650752 | tf_op jit(solution)/shard_map/all_gather | solution.py:48
  14.8 27.9 %all-to-all-start = ((f32[16,3,256]{2,1,0:T(4,128)}), f32[16,3,256]{2,1,0:T(4,128)S(1)}, u32[]{:S(2)}, u32[]{:S(2)}) async-start(f32[16,3,256]{2,1,0:T(4,128)} %broadcast_select_fusion.1), calls=%async_computation | async-start | bytes 131072 | tf_op jit(solution)/shard_map/all_to_all | solution.py:43
  33.5 16.4 %copy-start.5 = (f32[4]{0:T(128)S(1)}, f32[4]{0:T(128)}, u32[]{:S(2)}) copy-start(f32[4]{0:T(128)} %param.18) | copy-start | bytes 52
  33.5 16.4 %copy-start.1 = (f32[4,256]{1,0:T(4,128)S(1)}, f32[4,256]{1,0:T(4,128)}, u32[]{:S(2)}) copy-start(f32[4,256]{1,0:T(4,128)} %param.19) | copy-start | bytes 12292
  42.7 340.5 %all-to-all-start.1 = ((f32[16,4,64,256]{3,2,1,0:T(8,128)}), f32[16,4,64,256]{3,2,1,0:T(8,128)}, u32[]{:S(2)}, u32[]{:S(2)}) async-start(f32[16,4,64,256]{3,2,1,0:T(8,128)} %broadcast_select_fusion), calls=%async_computation.1 | async-start | bytes 8388608 | tf_op jit(solution)/shard_map/all_to_all | solution.py:42
  79.8 298.2 %copy-start.2 = (f32[4]{0:T(128)S(1)}, f32[4]{0:T(128)}, u32[]{:S(2)}) copy-start(f32[4]{0:T(128)} %param.17) | copy-start | bytes 52
  79.8 300.4 %copy-start.3 = (f32[256]{0:T(256)S(1)}, f32[256]{0:T(256)}, u32[]{:S(2)}) copy-start(f32[256]{0:T(256)} %param.20) | copy-start | bytes 3076
  381.0 2.2 copy-start.4
Sparse Core Ops, SparseCore 0:
  11.2 63.0 all-gather.7
  76.4 218.4 all-gather.3
  297.9 71.3 all-gather.5
where the time goes:
time: 398 us; the launch traced here: 395 us
  waiting for transfers between devices  324 us (81%)
  starting transfers between devices  19.9 us (5%)
  between operations  16.6 us (4%)
  matrix products  16.2 us (4%)
  other arithmetic  9.28 us (2%)
  local copies, waits for them, and re-layouts  9.1 us (2%)
    all_gather x1, waiting for transfers between devices, on_device(): lax.all_gather(joined_weight, 'rep', axis=0, tiled=True)  215 us
    all_gather x1, waiting for transfers between devices, on_device(): lax.all_gather(layer_input, 'head', axis=1, tiled=True)  74.4 us
    all_gather x1, waiting for transfers between devices, on_device(): lax.all_gather(group_inputs, 'head', axis=1, tiled=True)  24.2 us
    all_to_all x1, starting transfers between devices, on_device(): lax.all_to_all(send_tail, 'rep', split_axis=0, concat_axis=0, tiled=True)  15.2 us
    all_to_all x1, waiting for transfers between devices, on_device(): lax.all_to_all(send_tail, 'rep', split_axis=0, concat_axis=0, tiled=True)  9.18 us
    dot_general x1, matrix products, on_device(): jnp.dot(whole, lax.all_gather(joined_weight, 'rep', axis=0, tiled=True),...  8.69 us
  transfers between devices with their start and end apart: 5, of which 4 were waited for; matrix products, arithmetic and copies ran while one was open for 7% of the time, Pallas kernels for 0%

commit v1 on v0

v1 whole, which is shorter than its diff:
```python
import jax
import jax.numpy as jnp
from jax import lax
from jax.experimental import pallas as pl
from jax.experimental.pallas import tpu as pltpu
from jax.sharding import PartitionSpec as P

MESH = pl.DeviceIdType.MESH
BF = jnp.bfloat16
F32 = jnp.float32
Z = 16
TOK = 512
CH = 256
HEADS = 4
N = 256
WSUB = 4
SSUB = 2


def body(
    request_state, owner_map, shared_id, step_bias, decay_log, skip_gain,
    x_hbm, w_hbm, misc_in, state_hbm, g_hbm, conv_w, conv_b,
    out_ref, fstate_ref, ftail_ref,
    A, W, S, M, G, state_own, g_own, acc, sacc, ext, inT, outv, score, mix, xbd,
    loc_sem, ws_sem, wr_sem, ss_sem, sr_sem, ms_sem, mr_sem, as_sem, ar_sem, cs_sem, cr_sem, gs_sem, gr_sem,
):
    z = lax.axis_index("rep")
    hid = lax.axis_index("head")
    x, y, c = hid // 8, (hid // 2) % 4, hid % 2
    zr, zl = (z + 1) % Z, (z + Z - 1) % Z

    def dev(xx, yy, cc):
        return {"head": xx * 8 + yy * 2 + cc}

    xp, xm, yp, ym = (x + 1) % 4, (x + 3) % 4, (y + 1) % 4, (y + 3) % 4
    sibling = dev(x, y, 1 - c)
    zdev = ({"rep": zr}, {"rep": zl})
    pos = ((y, x), (x, y))
    x_nb, y_nb = (dev(xp, y, c), dev(xm, y, c)), (dev(x, yp, c), dev(x, ym, c))
    q_nb, p_nb = (x_nb, y_nb), (y_nb, x_nb)

    locs = [
        pltpu.make_async_copy(g_hbm, g_own, loc_sem.at[0]),
        pltpu.make_async_copy(x_hbm.at[0:256], A.at[0, c, y, x], loc_sem.at[1]),
        pltpu.make_async_copy(x_hbm.at[256:512], A.at[1, c, x, y], loc_sem.at[2]),
        pltpu.make_async_copy(w_hbm, W.at[0], loc_sem.at[3]),
        pltpu.make_async_copy(state_hbm, state_own, loc_sem.at[4]),
        pltpu.make_async_copy(misc_in, M.at[0], loc_sem.at[5]),
    ]
    for copy in locs:
        copy.start()

    barrier = pltpu.get_barrier_semaphore()
    for d in (*zdev, *x_nb, *y_nb, sibling):
        pl.semaphore_signal(barrier, inc=1, device_id=d, device_id_type=MESH)

    locs[0].wait()
    g_wide = jnp.concatenate([g_own[...].astype(F32), jnp.zeros((TOK, 64), F32)], axis=1)
    G[c, y] = g_wide.T[0:64].astype(BF)
    locs[4].wait()
    S[0] = state_own[...].astype(BF)
    for i in (1, 2, 3, 5):
        locs[i].wait()
    pl.semaphore_wait(barrier, 7)

    sends = []

    def rcopy(src, dst, s_sem, r_sem, d):
        return pltpu.make_async_remote_copy(
            src_ref=src, dst_ref=dst, send_sem=s_sem, recv_sem=r_sem, device_id=d, device_id_type=MESH
        )

    def go(ref, s_sem, r_sem, d, dst=None):
        copy = rcopy(ref, ref if dst is None else dst, s_sem, r_sem, d)
        copy.start()
        sends.append(copy)

    def got(ref, s_sem, r_sem, d):
        rcopy(ref, ref, s_sem, r_sem, d).wait_recv()

    def slot(way, s):
        return s if way == 0 else (Z - s) % Z

    def ring(buf, rows, sub, s_sem, r_sem, way, s):
        here = buf.at[slot(way, s), rows]
        if s > 0:
            got(here, s_sem.at[way, s - 1, sub], r_sem.at[way, s - 1, sub], zdev[way])
        if s < 8 and not (s == 7 and sub not in last_subs(way, s_sem)):
            go(here, s_sem.at[way, s, sub], r_sem.at[way, s, sub], zdev[way], buf.at[slot(way, s + 1), rows])

    def last_subs(way, s_sem):
        if s_sem is ws_sem:
            return (0, 1) if way == 0 else (2, 3)
        if s_sem is ss_sem:
            return (0,) if way == 0 else (1,)
        return (0,) if way == 0 else ()

    def w_step(s, subs=range(WSUB)):
        for sub in subs:
            for way in (0, 1):
                if s < 8 or sub in last_subs(way, ws_sem):
                    ring(W, pl.ds(sub * (512 // WSUB), 512 // WSUB), sub, ws_sem, wr_sem, way, s)

    def s_step(s, subs=range(SSUB)):
        for sub in subs:
            for way in (0, 1):
                if s < 8 or sub in last_subs(way, ss_sem):
                    ring(S, pl.ds(sub * (256 // SSUB), 256 // SSUB), sub, ss_sem, sr_sem, way, s)

    def m_step(s):
        for way in (0, 1):
            if s < 8 or 0 in last_subs(way, ms_sem):
                ring(M, pl.ds(0, 16), 0, ms_sem, mr_sem, way, s)

    def ring4(stage, blk, halves, nb, s_sem, r_sem):
        if stage == 0:
            for way in (0, 1):
                go(blk(0), s_sem.at[way], r_sem.at[way], nb[way])
        elif stage == 1:
            for way, step in ((0, -1), (1, 1)):
                got(blk(step), s_sem.at[way], r_sem.at[way], nb[way])
                go(halves(blk(step), way), s_sem.at[2 + way], r_sem.at[2 + way], nb[way])
        else:
            for way in (0, 1):
                got(halves(blk(2), way), s_sem.at[2 + way], r_sem.at[2 + way], nb[way])

    def a_one(stage, i):
        p, q = pos[i]
        ring4(
            stage,
            lambda k: A.at[i, c, p, (q + 4 + k) % 4],
            lambda ref, way: ref.at[pl.ds(128 * way, 128)],
            q_nb[i], as_sem.at[i, 0], ar_sem.at[i, 0],
        )

    def a_two(stage, i):
        p, _ = pos[i]
        ring4(
            stage,
            lambda k: A.at[i, c, (p + 4 + k) % 4],
            lambda ref, way: ref.at[pl.ds(2 * way, 2)],
            p_nb[i], as_sem.at[i, 1], ar_sem.at[i, 1],
        )

    def a_share(i, k):
        p, _ = pos[i]
        go(A.at[i, c, (p + k) % 4], cs_sem.at[i, k], cr_sem.at[i, k], sibling)

    def a_shared(i, k):
        p, _ = pos[i]
        got(A.at[i, 1 - c, (p + k) % 4], cs_sem.at[i, k], cr_sem.at[i, k], sibling)

    def g_ring(stage):
        ring4(
            stage,
            lambda k: G.at[c, (y + 4 + k) % 4],
            lambda ref, way: ref.at[pl.ds(32 * way, 32)],
            y_nb, gs_sem, gr_sem,
        )

    def a_block(i, kz, cc):
        ax, ay = kz // 4, kz % 4
        return A[0, cc, ay, ax] if i == 0 else A[1, cc, ax, ay]

    def project(j):
        kz = (z - j + Z) % Z
        for i in (0, 1):
            rows = pl.ds(256 * i, 256)
            part = jnp.dot(a_block(i, kz, 0), W[j, 0:256], preferred_element_type=F32)
            part += jnp.dot(a_block(i, kz, 1), W[j, 256:512], preferred_element_type=F32)
            acc[rows, :] += part

    def step_part(j):
        kz = (z - j + Z) % Z
        for i in (0, 1):
            for cc in (0, 1):
                sacc[cc, :, pl.ds(256 * i, 256)] += lax.dot_general(
                    M[j], a_block(i, kz, cc), (((1,), (1,)), ((), ())), preferred_element_type=F32
                )

    m_step(0)
    for i in (0, 1):
        a_one(0, i)
    g_ring(0)
    s_step(0)
    w_step(0)
    acc[...] = jnp.zeros_like(acc)
    sacc[...] = jnp.zeros_like(sacc)
    m_step(1)
    for i in (0, 1):
        a_one(1, i)
    g_ring(1)
    for i in (0, 1):
        a_one(2, i)
        a_two(0, i)
        a_share(i, 0)
    g_ring(2)
    go(G.at[c], gs_sem.at[4], gr_sem.at[4], sibling)
    m_step(2)
    s_step(1)
    w_step(1)
    m_step(3)
    got(G.at[1 - c], gs_sem.at[4], gr_sem.at[4], sibling)
    for k in range(4):
        inT[pl.ds(64 * k, 64), :] = G[k % 2, k // 2]
        outv[:, pl.ds(64 * k, 64)] = G[k % 2, 2 + k // 2].astype(F32).T.astype(BF)
    for tb in range(4):
        t0 = tb * 128
        cols = 256 if tb < 2 else 512
        sc = jnp.dot(outv[pl.ds(t0, 128), :], inT[:, 0:cols], preferred_element_type=F32)
        keep = lax.broadcasted_iota(jnp.int32, (128, cols), 1) <= t0 + lax.broadcasted_iota(jnp.int32, (128, cols), 0)
        score[pl.ds(t0, 128), 0:cols] = jnp.where(keep, sc, 0.0)
    m_step(4)
    for i in (0, 1):
        a_two(1, i)
        a_share(i, 3)
        a_share(i, 1)
    s_step(2)
    w_step(2)
    m_step(5)
    for i in (0, 1):
        a_two(2, i)
        a_share(i, 2)
    s_step(3)
    w_step(3)
    m_step(6)
    m_step(7)
    for i in (0, 1):
        for k in range(4):
            a_shared(i, k)
    s_step(4)
    w_step(4)
    m_step(8)

    @pl.loop(0, Z)
    def _(j):
        step_part(j)

    project(0)

    @pl.loop(1, 5)
    def _(j):
        project(j)
        project(Z - j)

    row = lax.broadcasted_iota(jnp.int32, (8, 1), 0)

    def per_head(ref):
        col = jnp.zeros((8, 1), F32)
        for h in range(HEADS):
            col = jnp.where(row == h, ref[h], col)
        return col

    raw = jnp.concatenate([sacc[0, 0:4] + sacc[1, 4:8], jnp.zeros((4, TOK), F32)], axis=0)
    raw = raw + per_head(step_bias)
    step = jnp.maximum(raw, 0.0) + jnp.log1p(jnp.exp(-jnp.abs(raw)))
    decay = -jnp.exp(per_head(decay_log)) * step
    lane = lax.broadcasted_iota(jnp.int32, (8, TOK), 1)
    for k in range(9):
        decay = decay + jnp.where(lane >= 2**k, pltpu.roll(decay, 2**k, axis=1), 0.0)
    last = decay[:, TOK - 1 : TOK]
    weights = jnp.exp(last - decay) * step
    decay_t = jnp.concatenate([decay, jnp.zeros((120, TOK), F32)], axis=0).T
    grown_t = jnp.exp(decay_t)
    weights_t = jnp.concatenate([weights, jnp.zeros((120, TOK), F32)], axis=0).T
    s_step(5)
    w_step(5)
    project(5)
    project(Z - 5)

    def make_mix(h):
        for tb in range(4):
            t0 = tb * 128
            cols = 256 if tb < 2 else 512
            differ = decay_t[t0 : t0 + 128, h : h + 1] - decay[h : h + 1, 0:cols]
            scaled = jnp.exp(jnp.minimum(differ, 0.0)) * step[h : h + 1, 0:cols]
            mix[h, pl.ds(t0, 128), 0:cols] = (score[pl.ds(t0, 128), 0:cols] * scaled).astype(BF)

    make_mix(0)
    make_mix(1)
    s_step(6)
    w_step(6)
    project(6)
    project(Z - 6)
    make_mix(2)
    make_mix(3)
    s_step(7)
    w_step(7)
    project(7)
    project(Z - 7)

    chan = lax.broadcasted_iota(jnp.int32, (TOK, CH), 1) // 64

    def expand(cols):
        wide = jnp.broadcast_to(cols[:, 0:1], (TOK, CH))
        for h in range(1, HEADS):
            wide = jnp.where(chan == h, cols[:, h : h + 1], wide)
        return wide

    grown = expand(grown_t)
    weigh = expand(weights_t)
    s_step(8)
    sid = request_state[z]
    sid = jnp.where(sid < Z, sid, shared_id[0])
    j_state = (z - owner_map[sid] + Z) % Z
    prior = S[j_state]
    base = lax.dot_general(outv[...], prior, (((1,), (1,)), ((), ())), preferred_element_type=F32) * grown
    ext[0:8, :] = jnp.concatenate([jnp.zeros((5, CH), F32), M[j_state].astype(F32)[8:11]], axis=0)

    w_step(8)
    project(8)
    projected = acc[...].astype(BF).astype(F32)
    ext[8 : 8 + TOK, :] = projected
    ftail_ref[...] = ext[TOK + 5 : TOK + 8, :]
    conv = conv_b[...] + conv_w[0:1, :] * ext[5 : 5 + TOK, :]
    for k in range(1, 4):
        conv = conv + conv_w[k : k + 1, :] * ext[5 + k : 5 + k + TOK, :]
    conv_f = (conv / (1.0 + jnp.exp(-conv))).astype(BF).astype(F32)
    skip = jnp.zeros((1, CH), F32)
    one = lax.broadcasted_iota(jnp.int32, (1, CH), 1) // 64
    for h in range(HEADS):
        skip = jnp.where(one == h, skip_gain[h], skip)
        xbd[h] = jnp.where(chan == h, conv_f, 0.0).astype(BF)
    rest = base + skip * conv_f
    for tb in range(2):
        rows = pl.ds(256 * tb, 256)
        cols = 256 * (tb + 1)
        inner = rest[256 * tb : 256 * tb + 256]
        for h in range(HEADS):
            inner = inner + jnp.dot(mix[h, rows, 0:cols], xbd[h, 0:cols, :], preferred_element_type=F32)
        out_ref[rows, :] = inner.astype(BF)
    weighted = (conv_f * weigh).astype(BF)
    new_t = jnp.dot(inT[...], weighted, preferred_element_type=F32)
    head_row = lax.broadcasted_iota(jnp.int32, (CH, 1), 0) // 64
    kept = jnp.zeros((CH, 1), F32)
    last_e = jnp.exp(last)
    for h in range(HEADS):
        kept = jnp.where(head_row == h, last_e[h : h + 1, 0:1], kept)
    fstate_ref[...] = kept * prior.astype(F32) + new_t.T

    for copy in sends:
        copy.wait_send()


def on_device(
    layer_input, proj_weight, step_weight, step_bias, decay_log, conv_weight, conv_bias, skip_gain,
    group_inputs, cached_state, cached_tail, owner_map, request_state, shared_id,
):
    sw = step_weight.T.reshape(4, 2, 256).transpose(1, 0, 2).reshape(8, 256)
    misc = jnp.concatenate([sw, cached_tail[0].astype(BF), jnp.zeros((5, CH), BF)], axis=0)
    smem = pl.BlockSpec(memory_space=pltpu.SMEM)
    vmem = pl.BlockSpec(memory_space=pltpu.VMEM)
    hbm = pl.BlockSpec(memory_space=pl.ANY)
    dma = pltpu.SemaphoreType.DMA
    out, fstate, ftail = pl.pallas_call(
        body,
        out_shape=(
            jax.ShapeDtypeStruct((TOK, CH), BF),
            jax.ShapeDtypeStruct((CH, N), F32),
            jax.ShapeDtypeStruct((3, CH), F32),
        ),
        in_specs=[smem] * 6 + [hbm] * 5 + [vmem] * 2,
        out_specs=(vmem, vmem, vmem),
        scratch_shapes=[
            pltpu.VMEM((2, 2, 4, 4, 256, 256), BF),
            pltpu.VMEM((Z, 512, 256), BF),
            pltpu.VMEM((Z, 256, 256), BF),
            pltpu.VMEM((Z, 16, 256), BF),
            pltpu.VMEM((2, 4, 64, 512), BF),
            pltpu.VMEM((256, 256), F32),
            pltpu.VMEM((512, 64), BF),
            pltpu.VMEM((512, 256), F32),
            pltpu.VMEM((2, 16, 512), F32),
            pltpu.VMEM((8 + TOK, 256), F32),
            pltpu.VMEM((256, 512), BF),
            pltpu.VMEM((512, 256), BF),
            pltpu.VMEM((512, 512), F32),
            pltpu.VMEM((4, 512, 512), BF),
            pltpu.VMEM((4, 512, 256), BF),
            dma((6,)),
            dma((2, 8, WSUB)),
            dma((2, 8, WSUB)),
            dma((2, 8, SSUB)),
            dma((2, 8, SSUB)),
            dma((2, 8, 1)),
            dma((2, 8, 1)),
            dma((2, 2, 4)),
            dma((2, 2, 4)),
            dma((2, 4)),
            dma((2, 4)),
            dma((5,)),
            dma((5,)),
        ],
        compiler_params=pltpu.CompilerParams(
            collective_id=0, has_side_effects=True, vmem_limit_bytes=56 * 1024 * 1024
        ),
    )(
        request_state, owner_map, shared_id, step_bias, decay_log, skip_gain,
        layer_input, proj_weight, misc, cached_state.reshape(CH, N), group_inputs,
        conv_weight, conv_bias.reshape(1, CH),
    )
    return out, fstate.reshape(1, HEADS, 64, N), ftail[None]


def solution(mesh):
    return jax.shard_map(
        on_device,
        mesh=mesh,
        in_specs=(
            P("rep", "head"), P("rep", "head"), P("rep", "head"), P("head"), P("head"), P(None, "head"),
            P("head"), P("head"), P("rep", "head"), P("rep", "head", None, None), P("rep", None, "head"),
            P(), P(), P(),
        ),
        out_specs=(P("rep", "head"), P("rep", "head", None, None), P("rep", None, "head")),
        check_vma=False,
    )
```

time: 398 us -> 96.6 us (0.24)
  waiting for transfers between devices: 324 us -> 0 us
  Pallas kernels: 0 us -> 87.4 us
  starting transfers between devices: 19.9 us -> 0 us
  matrix products: 16.2 us -> 0 us
  between operations: 16.6 us -> 1.32 us
  other arithmetic: 9.28 us -> 0.67 us
    all_gather x3 -> x0, waiting for transfers between devices: 314 us -> none  [the longest x1 215 us: on_device(): lax.all_gather(joined_weight, 'rep', axis=0, tiled=True)]
    pallas_call x0 -> x1, Pallas kernels: none -> 87.4 us  [on_device(): pl.pallas_call(body, out_shape=(jax.ShapeDtypeStruct((TOK, CH), BF), jax....]
    all_to_all x2 -> x0, starting transfers between devices: 19.8 us -> none  [the longest x1 15.2 us: on_device(): lax.all_to_all(send_tail, 'rep', split_axis=0, concat_axis=0, tiled=True)]
    dot_general x5 -> x0, matrix products: 16.2 us -> none  [the longest x1 8.69 us: on_device(): jnp.dot(whole, lax.all_gather(joined_weight, 'rep', axis=0, tiled=True),...]
    all_to_all x2 -> x0, waiting for transfers between devices: 9.18 us -> none  [the longest x1 9.18 us: on_device(): lax.all_to_all(send_tail, 'rep', split_axis=0, concat_axis=0, tiled=True)]
    select_n x4 -> x0, other arithmetic: 4.94 us -> none  [the longest x1 3.54 us: on_device(): send_state = jnp.where(needed[:, None, None, None], cached_state, 0.0)]
  transfers between devices with their start and end apart: 5 -> 0, of which waited for: 4 -> 0; matrix products, arithmetic and copies ran while one was open for 7% -> 0% of each run, Pallas kernels for 0% -> 0%
where the time goes in v1:
time: 96.6 us; the launch traced here: 95.3 us
  Pallas kernels  87.4 us (90%)
  local copies, waits for them, and re-layouts  5.96 us (6%)
  between operations  1.32 us (1%)
    pallas_call x1, Pallas kernels, on_device(): pl.pallas_call(body, out_shape=(jax.ShapeDtypeStruct((TOK, CH), BF), jax....  87.4 us
    unnamed x13, local copies, waits for them, and re-layouts  5.87 us

profile of v1, /device:TPU:6, one launch (start us, length us, event | category | flops | bytes accessed | tf_op | source)
XLA Modules:
  0.0 95.3 jit_solution(10824368903256888533)
XLA Ops:
  1.3 0.0 copy-start.3
  1.3 0.0 copy-start.2
  1.3 0.1 pad.2.clone
  1.4 0.6 copy-done.3
  2.0 0.0 copy-done.2
  2.0 0.7 maximum_maximum_fusion.misc_in
  2.7 1.6 %copy.19.g_hbm = bf16[512,64]{1,0:T(8,128)(2,1)} copy(bf16[512,64]{0,1:T(8,128)(2,1)} %param.22) | data formatting | bytes 131072 | tf_op args[8]
  4.3 87.4 %shard_map.157 = (bf16[512,256]{1,0:T(8,128)(2,1)}, f32[256,256]{1,0:T(8,128)}, f32[3,256]{1,0:T(4,128)}) custom-call(s32[16]{0:T(128)} %request_state.1, s32[16]{0:T(128)} %owner_map.1, s32[1]{0:T(128)S(6)} %copy.27.shared_id, f32[4]{0:T(128)} %step_bias.1, f32[4]{0:T(128)} %decay_log.1, f32[4]{0:T(128)} %skip_gain.1, bf16[512,256]{1,0:T(8,128)(2,1)} %x_hbm.1, ...), custom_call_target="tpu_custom_call" | custom-call | tf_op jit(solution)/shard_map/pallas_call | solution.py:355
  91.7 0.0 copy-start.1
  91.7 0.7 copy-done.1
  92.3 0.6 copy.20
  92.9 0.0 copy-start
  92.9 1.7 %copy.28 = bf16[512,256]{1,0:T(8,128)(2,1)} copy(bf16[512,256]{1,0:T(8,128)(2,1)} %get-tuple-element.15) | data formatting | bytes 524288
  94.6 0.0 copy-done
  94.6 0.7 copy.29
  (3 shorter events, 0.0 us)
Async XLA Ops:
  1.3 0.7 copy-start.3
  1.3 0.7 copy-start.2
  91.7 0.7 copy-start.1
  92.9 1.7 %copy-start = (f32[256,256]{1,0:T(8,128)S(1)}, f32[256,256]{1,0:T(8,128)}, u32[]{:S(2)}) copy-start(f32[256,256]{1,0:T(8,128)} %get-tuple-element.7) | copy-start | bytes 786436

commit v2 on v1

v2 whole, which is shorter than its diff:
```python
import functools

import jax
import jax.numpy as jnp
from jax import lax
from jax.experimental import pallas as pl
from jax.experimental.pallas import tpu as pltpu
from jax.sharding import PartitionSpec as P

MESH = pl.DeviceIdType.MESH
BF = jnp.bfloat16
F32 = jnp.float32
Z = 16
TOK = 512
CH = 256
HEADS = 4
N = 256
WSUB = 4
SSUB = 2
STEPS = 9
HELD = STEPS + 2
REACH = (9, 6)


def body(
    fast,
    request_state, owner_map, shared_id, step_bias, decay_log, skip_gain,
    x_hbm, w_hbm, sw_hbm, tail_hbm, state_hbm, g_hbm, conv_w, conv_b,
    out_ref, fstate_ref, ftail_ref, flag_ref,
    A, W, S, M, G, stage, landed, plan_v, plan, state_own, sw_own, tail_own, acc, sacc, ext, inT, outv, score, mix, xbd, rates, rate_t,
    loc_sem, ws_sem, wr_sem, ss_sem, sr_sem, ms_sem, mr_sem, as_sem, ar_sem, cs_sem, cr_sem, gs_sem, gr_sem, vs_sem, vr_sem, plan_sem,
):
    z = lax.axis_index("rep")
    hid = lax.axis_index("head")
    x, y, c = hid // 8, (hid // 2) % 4, hid % 2
    zr, zl = (z + 1) % Z, (z + Z - 1) % Z

    def dev(xx, yy, cc):
        return {"head": xx * 8 + yy * 2 + cc}

    xp, xm, yp, ym = (x + 1) % 4, (x + 3) % 4, (y + 1) % 4, (y + 3) % 4
    sibling = dev(x, y, 1 - c)
    zdev = ({"rep": zr}, {"rep": zl})
    pos = ((y, x), (x, y))
    x_nb, y_nb = (dev(xp, y, c), dev(xm, y, c)), (dev(x, yp, c), dev(x, ym, c))
    q_nb, p_nb = (x_nb, y_nb), (y_nb, x_nb)

    barrier = pltpu.get_barrier_semaphore()
    for d in (*zdev, *x_nb, *y_nb, sibling):
        pl.semaphore_signal(barrier, inc=1, device_id=d, device_id_type=MESH)

    locs = [
        pltpu.make_async_copy(sw_hbm, sw_own, loc_sem.at[0]),
        pltpu.make_async_copy(tail_hbm, tail_own, loc_sem.at[1]),
        pltpu.make_async_copy(state_hbm, state_own, loc_sem.at[2]),
        pltpu.make_async_copy(w_hbm, W.at[0], loc_sem.at[3]),
        pltpu.make_async_copy(x_hbm.at[0:256], A.at[0, c, y, x], loc_sem.at[4]),
        pltpu.make_async_copy(x_hbm.at[256:512], A.at[1, c, x, y], loc_sem.at[5]),
        pltpu.make_async_copy(g_hbm, G.at[c, y], loc_sem.at[6]),
    ]
    for copy in locs:
        copy.start()
    locs[0].wait()
    locs[1].wait()
    sw = sw_own[...].astype(F32)
    M[0] = jnp.concatenate(
        [sw[:, 0:256], sw[:, 256:512]] + [tail_own[k] for k in range(3)] + [jnp.zeros((5, CH), F32)], axis=0
    ).astype(BF)
    locs[2].wait()
    own = state_own[...].astype(BF)
    if fast:
        S[...] = jnp.zeros_like(S)
        for way in (0, 1):
            for part in (0, 1):
                S[way * HELD + part] = own[128 * part : 128 * part + 128]
    else:
        S[0] = own
    for i in range(3, 7):
        locs[i].wait()
    pl.semaphore_wait(barrier, 7)

    sends = []

    def rcopy(src, dst, s_sem, r_sem, d):
        return pltpu.make_async_remote_copy(
            src_ref=src, dst_ref=dst, send_sem=s_sem, recv_sem=r_sem, device_id=d, device_id_type=MESH
        )

    def go(ref, s_sem, r_sem, d, dst=None):
        copy = rcopy(ref, ref if dst is None else dst, s_sem, r_sem, d)
        copy.start()
        sends.append(copy)

    def got(ref, s_sem, r_sem, d):
        rcopy(ref, ref, s_sem, r_sem, d).wait_recv()

    def slot(way, s):
        return s if way == 0 else (Z - s) % Z

    def ring(buf, rows, sub, s_sem, r_sem, way, s):
        here = buf.at[slot(way, s), rows]
        if s > 0:
            got(here, s_sem.at[way, s - 1, sub], r_sem.at[way, s - 1, sub], zdev[way])
        if s < 8 and not (s == 7 and sub not in last_subs(way, s_sem)):
            go(here, s_sem.at[way, s, sub], r_sem.at[way, s, sub], zdev[way], buf.at[slot(way, s + 1), rows])

    def last_subs(way, s_sem):
        if s_sem is ws_sem:
            return (0, 1) if way == 0 else (2, 3)
        if s_sem is ss_sem:
            return (0,) if way == 0 else (1,)
        return (0,) if way == 0 else ()

    def w_step(s, subs=range(WSUB)):
        for sub in subs:
            for way in (0, 1):
                if s < 8 or sub in last_subs(way, ws_sem):
                    ring(W, pl.ds(sub * (512 // WSUB), 512 // WSUB), sub, ws_sem, wr_sem, way, s)

    def s_step(s, subs=range(SSUB)):
        for sub in subs:
            for way in (0, 1):
                if s < 8 or sub in last_subs(way, ss_sem):
                    ring(S, pl.ds(sub * (256 // SSUB), 256 // SSUB), sub, ss_sem, sr_sem, way, s)

    def state_row(q):
        sid = request_state[q]
        return owner_map[jnp.where(sid < Z, sid, shared_id[0])]

    def make_plan():
        pack = lax.broadcasted_iota(jnp.int32, (1, 64), 1)
        way, src, part = pack // 32, (pack % 32) // 2, pack % 2
        most = jnp.where(part == 0, REACH[0], REACH[1])
        togo = jnp.zeros((1, 64), jnp.int32)
        for q in range(Z):
            row = state_row(q)
            d = (q - row + Z) % Z
            ahead = jnp.where((d <= most) & (way == 0), d, 0)
            behind = jnp.where((d > most) & (way == 1), Z - d, 0)
            togo = jnp.maximum(togo, jnp.where(src == row, ahead + behind, 0))
        togo = togo.astype(F32)
        at = src
        name = (src * 2 + part + 1).astype(F32)
        code = (part + 1).astype(F32)
        order = pack.astype(F32)
        link_row = lax.broadcasted_iota(jnp.int32, (32, 64), 0)
        sent, came = [], []
        for t in range(STEPS):
            key = jnp.where(togo > 0.0, togo * 64.0 + order, 0.0)
            here = link_row == at + way * Z
            best = jnp.max(jnp.where(here, key, 0.0), axis=1, keepdims=True)
            wins = here & (key == best) & (key > 0.0)
            win = jnp.max(jnp.where(wins, 1.0, 0.0), axis=0, keepdims=True)
            then = jnp.where(way == 0, (at + 1) % Z, (at + Z - 1) % Z)
            sent.append(jnp.where(at == z, win * code, 0.0))
            came.append(jnp.where(then == z, win * name, 0.0))
            togo = togo - win
            code = jnp.where(win > 0.0, t + 3.0, code)
            at = jnp.where(win > 0.0, then, at)
        rest = [jnp.zeros((Z - STEPS, 64), F32)]
        sent, came = jnp.concatenate(sent + rest, axis=0), jnp.concatenate(came + rest, axis=0)
        half = lax.broadcasted_iota(jnp.int32, (Z, 64), 1) // 32
        lane = lax.broadcasted_iota(jnp.int32, (Z, 128), 1)
        table = jnp.zeros((Z, 128), F32)
        for k, (what, w) in enumerate(((sent, 0), (sent, 1), (came, 0), (came, 1))):
            column = jnp.max(jnp.where(half == w, what, 0.0), axis=1, keepdims=True)
            table = jnp.where(lane == k, column, table)
        table = jnp.where(lane == 4, jnp.max(togo, axis=1, keepdims=True), table)
        plan_v[...] = table.astype(jnp.int32)
        copy = pltpu.make_async_copy(plan_v, plan, plan_sem)
        copy.start()
        copy.wait()
        flag_ref[0] = plan[0, 4]

    def convey(t):
        for way in (0, 1):
            if t > 0:
                got(landed.at[way, t - 1], vs_sem.at[way, t - 1], vr_sem.at[way, t - 1], zdev[way])
                S[way * HELD + t + 1] = landed[way, t - 1]
            if t < STEPS:
                k = jnp.clip(plan[t, way] - 1, 0, HELD - 1)
                stage[way, t] = S[way * HELD + k]
                go(stage.at[way, t], vs_sem.at[way, t], vr_sem.at[way, t], zdev[way], landed.at[way, t])

    def prior_half(row, part):
        at = part
        for way in (0, 1):
            for t in range(STEPS):
                at = jnp.where(plan[t, 2 + way] == row * 2 + part + 1, way * HELD + t + 2, at)
        return S[at]

    def m_step(s):
        for way in (0, 1):
            if s < 8 or 0 in last_subs(way, ms_sem):
                ring(M, pl.ds(0, 16), 0, ms_sem, mr_sem, way, s)

    def ring4(stage, blk, halves, nb, s_sem, r_sem):
        if stage == 0:
            for way in (0, 1):
                go(blk(0), s_sem.at[way], r_sem.at[way], nb[way])
        elif stage == 1:
            for way, step in ((0, -1), (1, 1)):
                got(blk(step), s_sem.at[way], r_sem.at[way], nb[way])
                go(halves(blk(step), way), s_sem.at[2 + way], r_sem.at[2 + way], nb[way])
        else:
            for way in (0, 1):
                got(halves(blk(2), way), s_sem.at[2 + way], r_sem.at[2 + way], nb[way])

    def a_one(stage, i):
        p, q = pos[i]
        ring4(
            stage,
            lambda k: A.at[i, c, p, (q + 4 + k) % 4],
            lambda ref, way: ref.at[pl.ds(128 * way, 128)],
            q_nb[i], as_sem.at[i, 0], ar_sem.at[i, 0],
        )

    def a_two(stage, i):
        p, _ = pos[i]

        def part(k, piece):
            return A.at[i, c, (p + 4 + k) % 4, pl.ds(2 * piece, 2)]

        def sems(n, way):
            return as_sem.at[i, 1 + n, way], ar_sem.at[i, 1 + n, way]

        for way, step in ((0, -1), (1, 1)):
            d = p_nb[i][way]
            if stage == 0:
                go(part(0, way), *sems(0, way), d)
                go(part(0, 1 - way), *sems(1, way), d)
            elif stage == 1:
                got(part(step, way), *sems(0, way), d)
                go(part(step, way), *sems(2, way), d)
            elif stage == 2:
                got(part(step, 1 - way), *sems(1, way), d)
            else:
                got(part(2, way), *sems(2, way), d)

    def a_share(i, k):
        p, _ = pos[i]
        go(A.at[i, c, (p + k) % 4], cs_sem.at[i, k], cr_sem.at[i, k], sibling)

    def a_shared(i, k):
        p, _ = pos[i]
        got(A.at[i, 1 - c, (p + k) % 4], cs_sem.at[i, k], cr_sem.at[i, k], sibling)

    def g_ring(stage):
        ring4(
            stage,
            lambda k: G.at[c, (y + 4 + k) % 4],
            lambda ref, way: ref.at[pl.ds(32 * way, 32)],
            y_nb, gs_sem, gr_sem,
        )

    def a_block(i, kz, cc):
        ax, ay = kz // 4, kz % 4
        return A[0, cc, ay, ax] if i == 0 else A[1, cc, ax, ay]

    def project(j):
        kz = (z - j + Z) % Z
        for i in (0, 1):
            rows = pl.ds(256 * i, 256)
            part = jnp.dot(a_block(i, kz, 0), W[j, 0:256], preferred_element_type=F32)
            part += jnp.dot(a_block(i, kz, 1), W[j, 256:512], preferred_element_type=F32)
            acc[rows, :] += part

    def step_part(j):
        kz = (z - j + Z) % Z
        for i in (0, 1):
            for cc in (0, 1):
                sacc[cc, :, pl.ds(256 * i, 256)] += lax.dot_general(
                    M[j], a_block(i, kz, cc), (((1,), (1,)), ((), ())), preferred_element_type=F32
                )

    def vectors():
        for k in range(4):
            inT[pl.ds(64 * k, 64), :] = G[k % 2, k // 2]
            outv[:, pl.ds(64 * k, 64)] = G[k % 2, 2 + k // 2].astype(F32).T.astype(BF)

    def scores(tb):
        t0 = tb * 128
        cols = 256 if tb < 2 else 512
        sc = jnp.dot(outv[pl.ds(t0, 128), :], inT[:, 0:cols], preferred_element_type=F32)
        keep = lax.broadcasted_iota(jnp.int32, (128, cols), 1) <= t0 + lax.broadcasted_iota(jnp.int32, (128, cols), 0)
        score[pl.ds(t0, 128), 0:cols] = jnp.where(keep, sc, 0.0)

    def decays():
        row = lax.broadcasted_iota(jnp.int32, (8, 1), 0)

        def per_head(ref):
            col = jnp.zeros((8, 1), F32)
            for h in range(HEADS):
                col = jnp.where(row == h, ref[h], col)
            return col

        raw = jnp.concatenate([sacc[0, 0:4] + sacc[1, 4:8], jnp.zeros((4, TOK), F32)], axis=0)
        raw = raw + per_head(step_bias)
        step = jnp.maximum(raw, 0.0) + jnp.log1p(jnp.exp(-jnp.abs(raw)))
        decay = -jnp.exp(per_head(decay_log)) * step
        lane = lax.broadcasted_iota(jnp.int32, (8, TOK), 1)
        for k in range(9):
            decay = decay + jnp.where(lane >= 2**k, pltpu.roll(decay, 2**k, axis=1), 0.0)
        last = decay[:, TOK - 1 : TOK]
        weights = jnp.exp(last - decay) * step
        rates[0] = decay
        rates[1] = step
        decay_t = jnp.concatenate([decay, jnp.zeros((120, TOK), F32)], axis=0).T
        grown_t = jnp.exp(decay_t)
        weights_t = jnp.concatenate([weights, jnp.zeros((120, TOK), F32)], axis=0).T
        rate_t[0] = decay_t
        rate_t[1] = grown_t
        rate_t[2] = weights_t

    def make_mix(h):
        for tb in range(4):
            t0 = tb * 128
            cols = 256 if tb < 2 else 512
            differ = rate_t[0, t0 : t0 + 128, h : h + 1] - rates[0, h : h + 1, 0:cols]
            scaled = jnp.exp(jnp.minimum(differ, 0.0)) * rates[1, h : h + 1, 0:cols]
            mix[h, pl.ds(t0, 128), 0:cols] = (score[pl.ds(t0, 128), 0:cols] * scaled).astype(BF)

    def step_parts(first):
        @pl.loop(first, first + 4)
        def _(j):
            step_part(j)

    def projects(first, end):
        @pl.loop(first, end)
        def _(j):
            project(j)
            project(Z - j)

    def g_share():
        go(G.at[c], gs_sem.at[4], gr_sem.at[4], sibling)

    def g_shared():
        got(G.at[1 - c], gs_sem.at[4], gr_sem.at[4], sibling)

    def both(f, *args):
        for i in (0, 1):
            f(*args, i)

    def shared(i):
        for k in range(4):
            a_shared(i, k)

    def clear():
        acc[...] = jnp.zeros_like(acc)
        sacc[...] = jnp.zeros_like(sacc)

    work = {u: [] for u in range(4 * 9)}

    def add(u, f, *args):
        work[u].append((f, args))

    if fast:
        for t in range(1, STEPS + 1):
            add(2 + 31 * t // STEPS, convey, t)
    else:
        for s in range(1, 9):
            add(4 * s, s_step, s)
    for s, u in enumerate((0, 4, 6, 8, 10, 13, 15, 18, 20)):
        if s:
            add(u, m_step, s)
    add(3, clear)
    add(5, both, a_one, 1)
    add(5, g_ring, 1)
    add(7, g_ring, 2)
    add(7, g_share)
    add(8, both, a_one, 2)
    add(8, both, a_two, 0)
    add(8, lambda: both(lambda i: a_share(i, 0)))
    add(11, g_shared)
    add(11, vectors)
    add(13, both, a_two, 1)
    for tb in range(4):
        add(12 + tb, scores, tb)
    add(16, both, a_two, 2)
    add(16, lambda: both(lambda i: (a_share(i, 3), a_share(i, 1))))
    add(19, both, a_two, 3)
    add(19, lambda: both(lambda i: a_share(i, 2)))
    add(21, both, shared)
    for k in range(4):
        add(21 + k, step_parts, 4 * k)
    add(24, decays)
    for h in range(HEADS):
        add(25 + h, make_mix, h)
    add(28, project, 0)
    add(29, projects, 1, 3)
    add(30, projects, 3, 5)
    add(31, projects, 5, 7)
    add(32, projects, 7, 8)

    m_step(0)
    both(a_one, 0)
    w_step(0, (0, 1))
    if fast:
        make_plan()
        convey(0)
    else:
        s_step(0)
    w_step(0, (2, 3))
    g_ring(0)
    for u in range(3, 36):
        if u > 3:
            w_step(u // 4, (u % 4,))
        for f, args in work[u]:
            f(*args)

    chan = lax.broadcasted_iota(jnp.int32, (TOK, CH), 1) // 64

    def expand(cols):
        wide = jnp.broadcast_to(cols[:, 0:1], (TOK, CH))
        for h in range(1, HEADS):
            wide = jnp.where(chan == h, cols[:, h : h + 1], wide)
        return wide

    grown = expand(rate_t[1])
    weigh = expand(rate_t[2])
    row = state_row(z)
    j_state = (z - row + Z) % Z
    if fast:
        prior = jnp.concatenate([prior_half(row, 0), prior_half(row, 1)], axis=0)
    else:
        prior = S[j_state]
    base = lax.dot_general(outv[...], prior, (((1,), (1,)), ((), ())), preferred_element_type=F32) * grown
    ext[0:8, :] = jnp.concatenate([jnp.zeros((5, CH), F32), M[j_state].astype(F32)[8:11]], axis=0)

    project(8)
    projected = acc[...].astype(BF).astype(F32)
    ext[8 : 8 + TOK, :] = projected
    for k in range(3):
        ftail_ref[k] = ext[TOK + 5 + k : TOK + 6 + k, :]
    conv = conv_b[...] + conv_w[0:1, :] * ext[5 : 5 + TOK, :]
    for k in range(1, 4):
        conv = conv + conv_w[k : k + 1, :] * ext[5 + k : 5 + k + TOK, :]
    conv_f = (conv / (1.0 + jnp.exp(-conv))).astype(BF).astype(F32)
    skip = jnp.zeros((1, CH), F32)
    one = lax.broadcasted_iota(jnp.int32, (1, CH), 1) // 64
    for h in range(HEADS):
        skip = jnp.where(one == h, skip_gain[h], skip)
        xbd[h] = jnp.where(chan == h, conv_f, 0.0).astype(BF)
    rest = base + skip * conv_f
    for tb in range(2):
        rows = pl.ds(256 * tb, 256)
        cols = 256 * (tb + 1)
        inner = rest[256 * tb : 256 * tb + 256]
        for h in range(HEADS):
            inner = inner + jnp.dot(mix[h, rows, 0:cols], xbd[h, 0:cols, :], preferred_element_type=F32)
        out_ref[rows, :] = inner.astype(BF)
    weighted = (conv_f * weigh).astype(BF)
    new_t = jnp.dot(inT[...], weighted, preferred_element_type=F32)
    head_row = lax.broadcasted_iota(jnp.int32, (CH, 1), 0) // 64
    kept = jnp.zeros((CH, 1), F32)
    last_e = jnp.exp(rates[0, :, TOK - 1 : TOK])
    for h in range(HEADS):
        kept = jnp.where(head_row == h, last_e[h : h + 1, 0:1], kept)
    fstate_ref[...] = kept * prior.astype(F32) + new_t.T

    for copy in sends:
        copy.wait_send()
    if not fast:
        flag_ref[0] = 0


def put(*refs):
    srcs, dsts, mids, sem = refs[0:3], refs[3:6], refs[6:9], refs[9]
    gets = [pltpu.make_async_copy(src, mid, sem.at[k]) for k, (src, mid) in enumerate(zip(srcs, mids))]
    puts = [pltpu.make_async_copy(mid, dst, sem.at[3 + k]) for k, (mid, dst) in enumerate(zip(mids, dsts))]
    for get in gets:
        get.start()
    for get, one in zip(gets, puts):
        get.wait()
        one.start()
    for one in puts:
        one.wait()


def on_device(
    layer_input, proj_weight, step_weight, step_bias, decay_log, conv_weight, conv_bias, skip_gain,
    group_inputs, cached_state, cached_tail, owner_map, request_state, shared_id,
):
    smem = pl.BlockSpec(memory_space=pltpu.SMEM)
    vmem = pl.BlockSpec(memory_space=pltpu.VMEM)
    hbm = pl.BlockSpec(memory_space=pl.ANY)
    dma = pltpu.SemaphoreType.DMA
    shapes = (
        jax.ShapeDtypeStruct((TOK, CH), BF),
        jax.ShapeDtypeStruct((CH, N), F32),
        jax.ShapeDtypeStruct((3, 1, CH), F32),
    )
    args = (
        request_state, owner_map, shared_id, step_bias, decay_log, skip_gain,
        layer_input, proj_weight, step_weight.T, cached_tail.transpose(1, 0, 2), cached_state.reshape(CH, N), group_inputs.T,
        conv_weight, conv_bias.reshape(1, CH),
    )

    def layer(fast):
        return pl.pallas_call(
            functools.partial(body, fast),
            out_shape=(*shapes, jax.ShapeDtypeStruct((1,), jnp.int32)),
            in_specs=[smem] * 6 + [hbm] * 6 + [vmem] * 2,
            out_specs=(vmem, vmem, vmem, smem),
            scratch_shapes=[
                pltpu.VMEM((2, 2, 4, 4, 256, 256), BF),
                pltpu.VMEM((Z, 512, 256), BF),
                pltpu.VMEM((2 * HELD, 128, 256) if fast else (Z, 256, 256), BF),
                pltpu.VMEM((Z, 16, 256), BF),
                pltpu.VMEM((2, 4, 64, 512), BF),
                pltpu.VMEM((2, STEPS, 128, 256), BF),
                pltpu.VMEM((2, STEPS, 128, 256), BF),
                pltpu.VMEM((Z, 128), jnp.int32),
                pltpu.SMEM((Z, 128), jnp.int32),
                pltpu.VMEM((256, 256), F32),
                pltpu.VMEM((4, 512), BF),
                pltpu.VMEM((3, 1, 256), F32),
                pltpu.VMEM((512, 256), F32),
                pltpu.VMEM((2, 16, 512), F32),
                pltpu.VMEM((8 + TOK, 256), F32),
                pltpu.VMEM((256, 512), BF),
                pltpu.VMEM((512, 256), BF),
                pltpu.VMEM((512, 512), F32),
                pltpu.VMEM((4, 512, 512), BF),
                pltpu.VMEM((4, 512, 256), BF),
                pltpu.VMEM((2, 8, 512), F32),
                pltpu.VMEM((3, 512, 128), F32),
                dma((7,)),
                dma((2, 8, WSUB)),
                dma((2, 8, WSUB)),
                dma((2, 8, SSUB)),
                dma((2, 8, SSUB)),
                dma((2, 8, 1)),
                dma((2, 8, 1)),
                dma((2, 4, 4)),
                dma((2, 4, 4)),
                dma((2, 4)),
                dma((2, 4)),
                dma((5,)),
                dma((5,)),
                dma((2, STEPS)),
                dma((2, STEPS)),
                dma,
            ],
            compiler_params=pltpu.CompilerParams(
                collective_id=0 if fast else 1, has_side_effects=True, vmem_limit_bytes=56 * 1024 * 1024
            ),
        )(*args)

    *results, left = layer(True)

    def place(*values):
        return pl.pallas_call(
            put,
            out_shape=shapes,
            in_specs=[hbm] * 3,
            out_specs=[hbm] * 3,
            scratch_shapes=[pltpu.VMEM(v.shape, v.dtype) for v in shapes] + [dma((6,))],
            compiler_params=pltpu.CompilerParams(vmem_limit_bytes=60 * 1024 * 1024),
        )(*values)

    def again(*_):
        return tuple(layer(False)[0:3])

    out, fstate, ftail = lax.cond(left[0] == 0, place, again, *results)
    return out, fstate.reshape(1, HEADS, 64, N), ftail.transpose(1, 0, 2)


def solution(mesh):
    return jax.shard_map(
        on_device,
        mesh=mesh,
        in_specs=(
            P("rep", "head"), P("rep", "head"), P("rep", "head"), P("head"), P("head"), P(None, "head"),
            P("head"), P("head"), P("rep", "head"), P("rep", "head", None, None), P("rep", None, "head"),
            P(), P(), P(),
        ),
        out_specs=(P("rep", "head"), P("rep", "head", None, None), P("rep", None, "head")),
        check_vma=False,
    )
```

time: 96.6 us -> 82.1 us (0.85); the launches traced: 95.3 us -> 81.9 us
  Pallas kernels: 87.4 us -> 76.4 us
  local copies, waits for them, and re-layouts: 5.96 us -> 3.3 us
    pallas_call x1 -> x2, Pallas kernels: 87.4 us -> 76.4 us  [the longest x1 76.3 us: layer(): pl.pallas_call(functools.partial(body, fast), out_shape=(*shapes, jax.Sha...]
    unnamed x13 -> x29, local copies, waits for them, and re-layouts: 5.87 us -> 3.3 us
where the time goes in v2:
time: 82.1 us; the launch traced here: 81.9 us
  Pallas kernels  76.4 us (93%)
  local copies, waits for them, and re-layouts  3.3 us (4%)
  between operations  2.14 us (3%)
    pallas_call x1, Pallas kernels, layer(): pl.pallas_call(functools.partial(body, fast), out_shape=(*shapes, jax.Sha...  76.3 us
    unnamed x29, local copies, waits for them, and re-layouts  3.3 us

profile of v2, /device:TPU:6, one launch (start us, length us, event | category | flops | bytes accessed | tf_op | source)
XLA Modules:
  0.0 81.9 jit_solution(17890106099072435893)
XLA Ops:
  0.6 0.0 copy-start.7
  0.6 0.0 copy-start.8
  0.7 0.0 copy-start.9
  1.3 0.0 copy-start.6
  1.3 0.0 copy-start.5
  1.4 0.0 copy-start.4
  1.4 0.0 copy-done.7
  1.4 0.0 copy-done.8
  1.4 0.0 copy-done.9
  1.4 0.6 copy-done.6
  2.0 0.0 copy-done.5
  2.0 0.0 copy-done.4
  2.1 0.0 copy-start
  2.1 0.0 copy-start.1
  2.1 0.0 copy-start.2
  2.1 0.0 copy-start.3
  2.1 76.3 %shard_map.157 = (bf16[512,256]{1,0:T(8,128)(2,1)S(1)}, f32[256,256]{1,0:T(8,128)S(1)}, f32[3,1,256]{2,1,0:T(1,128)S(1)}, s32[1]{0:T(128)}) custom-call(s32[16]{0:T(128)S(1)} %copy-done.8, s32[16]{0:T(128)S(1)} %copy-done.9, s32[1]{0:T(128)S(6)} %copy.26.shared_id, f32[4]{0:T(128)} %step_bias.1, f32[4]{0:T(128)} %decay_log.1, f32[4]{0:T(128)} %skip_gain.1, ...), custom_call_target="tpu_custom_call" | custom-call | tf_op jit(solution)/shard_map/pallas_call | solution.py:500
  79.0 0.0 copy-start.10
  79.1 0.0 copy-start.11
  79.1 0.0 copy-start.12
  79.1 0.0 copy-done
  79.1 0.0 copy-done.1
  79.1 0.0 copy-done.2
  79.1 0.0 copy-done.3
  79.1 0.6 copy-done.10
  79.7 0.0 copy-done.11
  79.7 0.0 copy-done.12
  79.7 0.1 conditional.1
  79.7 0.1 branch_1_fun.1
  79.9 0.7 copy.27
  80.6 0.7 copy.28
  81.3 0.6 copy.29
Async XLA Ops:
  0.6 0.7 copy-start.7
  0.6 0.7 copy-start.8
  0.7 0.7 copy-start.9
  1.3 0.7 copy-start.6
  1.3 0.7 copy-start.5
  1.4 0.7 copy-start.4
  2.1 77.0 %copy-start = (bf16[512,256]{1,0:T(8,128)(2,1)S(1)}, bf16[512,256]{1,0:T(8,128)(2,1)}, u32[]{:S(2)}) copy-start(bf16[512,256]{1,0:T(8,128)(2,1)} %x_hbm.1) | copy-start | bytes 786436
  2.1 77.0 %copy-start.1 = (bf16[512,256]{1,0:T(8,128)(2,1)S(1)}, bf16[512,256]{1,0:T(8,128)(2,1)}, u32[]{:S(2)}) copy-start(bf16[512,256]{1,0:T(8,128)(2,1)} %w_hbm.1) | copy-start | bytes 786436
  2.1 77.0 %copy-start.2 = (f32[1,4,64,256]{3,2,1,0:T(8,128)S(1)}, f32[1,4,64,256]{3,2,1,0:T(8,128)}, u32[]{:S(2)}) copy-start(f32[1,4,64,256]{3,2,1,0:T(8,128)} %param.25) | copy-start | bytes 786436
  2.1 77.1 %copy-start.3 = (bf16[512,64]{0,1:T(8,128)(2,1)S(1)}, bf16[512,64]{0,1:T(8,128)(2,1)}, u32[]{:S(2)}) copy-start(bf16[512,64]{0,1:T(8,128)(2,1)} %param.24) | copy-start | bytes 196612
  79.0 0.7 copy-start.10
  79.1 0.7 copy-start.11
  79.1 0.7 copy-start.12

commit v3 on v2

--- a/solution.py
+++ b/solution.py
@@ -1,5 +1,3 @@
-import functools
-
 import jax
 import jax.numpy as jnp
 from jax import lax
@@ -16,19 +14,17 @@
 HEADS = 4
 N = 256
 WSUB = 4
-SSUB = 2
-STEPS = 9
+STEPS = 10
 HELD = STEPS + 2
-REACH = (9, 6)
+REACH = (10, 5)
 
 
 def body(
-    fast,
     request_state, owner_map, shared_id, step_bias, decay_log, skip_gain,
     x_hbm, w_hbm, sw_hbm, tail_hbm, state_hbm, g_hbm, conv_w, conv_b,
-    out_ref, fstate_ref, ftail_ref, flag_ref,
-    A, W, S, M, G, stage, landed, plan_v, plan, state_own, sw_own, tail_own, acc, sacc, ext, inT, outv, score, mix, xbd, rates, rate_t,
-    loc_sem, ws_sem, wr_sem, ss_sem, sr_sem, ms_sem, mr_sem, as_sem, ar_sem, cs_sem, cr_sem, gs_sem, gr_sem, vs_sem, vr_sem, plan_sem,
+    out_ref, fstate_ref, ftail_ref,
+    A, W, S, M, G, stage, landed, plan_v, plan, state_own, sw_own, tail_own, acc, sacc, ext, inT, outv, score, mix, xbd, rates, rate_t, base, weigh, carry,
+    loc_sem, ws_sem, wr_sem, ms_sem, mr_sem, as_sem, ar_sem, cs_sem, cr_sem, gs_sem, gr_sem, vs_sem, vr_sem, plan_sem,
 ):
     z = lax.axis_index("rep")
     hid = lax.axis_index("head")
@@ -48,6 +44,49 @@
     barrier = pltpu.get_barrier_semaphore()
     for d in (*zdev, *x_nb, *y_nb, sibling):
         pl.semaphore_signal(barrier, inc=1, device_id=d, device_id_type=MESH)
+
+    sends = []
+
+    def rcopy(src, dst, s_sem, r_sem, d):
+        return pltpu.make_async_remote_copy(
+            src_ref=src, dst_ref=dst, send_sem=s_sem, recv_sem=r_sem, device_id=d, device_id_type=MESH
+        )
+
+    def go(ref, s_sem, r_sem, d, dst=None):
+        copy = rcopy(ref, ref if dst is None else dst, s_sem, r_sem, d)
+        copy.start()
+        sends.append(copy)
+
+    def got(ref, s_sem, r_sem, d):
+        rcopy(ref, ref, s_sem, r_sem, d).wait_recv()
+
+    def slot(way, s):
+        return s if way == 0 else (Z - s) % Z
+
+    def ring(buf, rows, sub, s_sem, r_sem, way, s):
+        here = buf.at[slot(way, s), rows]
+        if s > 0:
+            got(here, s_sem.at[way, s - 1, sub], r_sem.at[way, s - 1, sub], zdev[way])
+        if s < 8 and not (s == 7 and sub not in last_subs(way, s_sem)):
+            go(here, s_sem.at[way, s, sub], r_sem.at[way, s, sub], zdev[way], buf.at[slot(way, s + 1), rows])
+
+    def last_subs(way, s_sem):
+        if s_sem is ws_sem:
+            return (0, 1) if way == 0 else (2, 3)
+        return (0,) if way == 0 else ()
+
+    def w_step(s, subs=range(WSUB)):
+        for sub in subs:
+            for way in (0, 1):
+                if s < 8 or sub in last_subs(way, ws_sem):
+                    ring(W, pl.ds(sub * (512 // WSUB), 512 // WSUB), sub, ws_sem, wr_sem, way, s)
+
+    def early():
+        pl.semaphore_wait(barrier, 7)
+        for sub in (0, 1):
+            rows = pl.ds(128 * sub, 128)
+            for way in (0, 1):
+                go(w_hbm.at[rows], ws_sem.at[way, 0, sub], wr_sem.at[way, 0, sub], zdev[way], W.at[slot(way, 1), rows])
 
     locs = [
         pltpu.make_async_copy(sw_hbm, sw_own, loc_sem.at[0]),
@@ -60,6 +99,7 @@
     ]
     for copy in locs:
         copy.start()
+    early()
     locs[0].wait()
     locs[1].wait()
     sw = sw_own[...].astype(F32)
@@ -68,60 +108,12 @@
     ).astype(BF)
     locs[2].wait()
     own = state_own[...].astype(BF)
-    if fast:
-        S[...] = jnp.zeros_like(S)
-        for way in (0, 1):
-            for part in (0, 1):
-                S[way * HELD + part] = own[128 * part : 128 * part + 128]
-    else:
-        S[0] = own
+    S[...] = jnp.zeros_like(S)
+    for way in (0, 1):
+        for part in (0, 1):
+            S[way * HELD + part] = own[128 * part : 128 * part + 128]
     for i in range(3, 7):
         locs[i].wait()
-    pl.semaphore_wait(barrier, 7)
-
-    sends = []
-
-    def rcopy(src, dst, s_sem, r_sem, d):
-        return pltpu.make_async_remote_copy(
-            src_ref=src, dst_ref=dst, send_sem=s_sem, recv_sem=r_sem, device_id=d, device_id_type=MESH
-        )
-
-    def go(ref, s_sem, r_sem, d, dst=None):
-        copy = rcopy(ref, ref if dst is None else dst, s_sem, r_sem, d)
-        copy.start()
-        sends.append(copy)
-
-    def got(ref, s_sem, r_sem, d):
-        rcopy(ref, ref, s_sem, r_sem, d).wait_recv()
-
-    def slot(way, s):
-        return s if way == 0 else (Z - s) % Z
-
-    def ring(buf, rows, sub, s_sem, r_sem, way, s):
-        here = buf.at[slot(way, s), rows]
-        if s > 0:
-            got(here, s_sem.at[way, s - 1, sub], r_sem.at[way, s - 1, sub], zdev[way])
-        if s < 8 and not (s == 7 and sub not in last_subs(way, s_sem)):
-            go(here, s_sem.at[way, s, sub], r_sem.at[way, s, sub], zdev[way], buf.at[slot(way, s + 1), rows])
-
-    def last_subs(way, s_sem):
-        if s_sem is ws_sem:
-            return (0, 1) if way == 0 else (2, 3)
-        if s_sem is ss_sem:
-            return (0,) if way == 0 else (1,)
-        return (0,) if way == 0 else ()
-
-    def w_step(s, subs=range(WSUB)):
-        for sub in subs:
-            for way in (0, 1):
-                if s < 8 or sub in last_subs(way, ws_sem):
-                    ring(W, pl.ds(sub * (512 // WSUB), 512 // WSUB), sub, ws_sem, wr_sem, way, s)
-
-    def s_step(s, subs=range(SSUB)):
-        for sub in subs:
-            for way in (0, 1):
-                if s < 8 or sub in last_subs(way, ss_sem):
-                    ring(S, pl.ds(sub * (256 // SSUB), 256 // SSUB), sub, ss_sem, sr_sem, way, s)
 
     def state_row(q):
         sid = request_state[q]
@@ -165,12 +157,10 @@
         for k, (what, w) in enumerate(((sent, 0), (sent, 1), (came, 0), (came, 1))):
             column = jnp.max(jnp.where(half == w, what, 0.0), axis=1, keepdims=True)
             table = jnp.where(lane == k, column, table)
-        table = jnp.where(lane == 4, jnp.max(togo, axis=1, keepdims=True), table)
         plan_v[...] = table.astype(jnp.int32)
         copy = pltpu.make_async_copy(plan_v, plan, plan_sem)
         copy.start()
         copy.wait()
-        flag_ref[0] = plan[0, 4]
 
     def convey(t):
         for way in (0, 1):
@@ -345,21 +335,42 @@
         for k in range(4):
             a_shared(i, k)
 
+    chan = lax.broadcasted_iota(jnp.int32, (TOK, CH), 1) // 64
+
     def clear():
         acc[...] = jnp.zeros_like(acc)
         sacc[...] = jnp.zeros_like(sacc)
 
+    def expand(cols):
+        wide = jnp.broadcast_to(cols[:, 0:1], (TOK, CH))
+        for h in range(1, HEADS):
+            wide = jnp.where(chan == h, cols[:, h : h + 1], wide)
+        return wide
+
+    def expand_decays():
+        base[...] = expand(rate_t[1])
+        weigh[...] = expand(rate_t[2])
+
+    def resume():
+        row = state_row(z)
+        j_state = (z - row + Z) % Z
+        prior = jnp.concatenate([prior_half(row, 0), prior_half(row, 1)], axis=0)
+        base[...] *= lax.dot_general(outv[...], prior, (((1,), (1,)), ((), ())), preferred_element_type=F32)
+        ext[0:8, :] = jnp.concatenate([jnp.zeros((5, CH), F32), M[j_state].astype(F32)[8:11]], axis=0)
+        head_row = lax.broadcasted_iota(jnp.int32, (CH, 1), 0) // 64
+        kept = jnp.zeros((CH, 1), F32)
+        last_e = jnp.exp(rates[0, :, TOK - 1 : TOK])
+        for h in range(HEADS):
+            kept = jnp.where(head_row == h, last_e[h : h + 1, 0:1], kept)
+        carry[...] = kept * prior.astype(F32)
+
     work = {u: [] for u in range(4 * 9)}
 
     def add(u, f, *args):
         work[u].append((f, args))
 
-    if fast:
-        for t in range(1, STEPS + 1):
-            add(2 + 31 * t // STEPS, convey, t)
-    else:
-        for s in range(1, 9):
-            add(4 * s, s_step, s)
+    for t in range(1, STEPS + 1):
+        add(2 + 30 * t // STEPS, convey, t)
     for s, u in enumerate((0, 4, 6, 8, 10, 13, 15, 18, 20)):
         if s:
             add(u, m_step, s)
@@ -386,20 +397,18 @@
     add(24, decays)
     for h in range(HEADS):
         add(25 + h, make_mix, h)
+    add(28, expand_decays)
     add(28, project, 0)
     add(29, projects, 1, 3)
     add(30, projects, 3, 5)
     add(31, projects, 5, 7)
     add(32, projects, 7, 8)
+    add(32, resume)
 
     m_step(0)
     both(a_one, 0)
-    w_step(0, (0, 1))
-    if fast:
-        make_plan()
-        convey(0)
-    else:
-        s_step(0)
+    make_plan()
+    convey(0)
     w_step(0, (2, 3))
     g_ring(0)
     for u in range(3, 36):
@@ -407,25 +416,6 @@
             w_step(u // 4, (u % 4,))
         for f, args in work[u]:
             f(*args)
-
-    chan = lax.broadcasted_iota(jnp.int32, (TOK, CH), 1) // 64
-
-    def expand(cols):
-        wide = jnp.broadcast_to(cols[:, 0:1], (TOK, CH))
-        for h in range(1, HEADS):
-            wide = jnp.where(chan == h, cols[:, h : h + 1], wide)
-        return wide
-
-    grown = expand(rate_t[1])
-    weigh = expand(rate_t[2])
-    row = state_row(z)
-    j_state = (z - row + Z) % Z
-    if fast:
-        prior = jnp.concatenate([prior_half(row, 0), prior_half(row, 1)], axis=0)
-    else:
-        prior = S[j_state]
-    base = lax.dot_general(outv[...], prior, (((1,), (1,)), ((), ())), preferred_element_type=F32) * grown
-    ext[0:8, :] = jnp.concatenate([jnp.zeros((5, CH), F32), M[j_state].astype(F32)[8:11]], axis=0)
 
     project(8)
     projected = acc[...].astype(BF).astype(F32)
@@ -441,7 +431,7 @@
     for h in range(HEADS):
         skip = jnp.where(one == h, skip_gain[h], skip)
         xbd[h] = jnp.where(chan == h, conv_f, 0.0).astype(BF)
-    rest = base + skip * conv_f
+    rest = base[...] + skip * conv_f
     for tb in range(2):
         rows = pl.ds(256 * tb, 256)
         cols = 256 * (tb + 1)
@@ -449,32 +439,21 @@
         for h in range(HEADS):
             inner = inner + jnp.dot(mix[h, rows, 0:cols], xbd[h, 0:cols, :], preferred_element_type=F32)
         out_ref[rows, :] = inner.astype(BF)
-    weighted = (conv_f * weigh).astype(BF)
+    weighted = (conv_f * weigh[...]).astype(BF)
     new_t = jnp.dot(inT[...], weighted, preferred_element_type=F32)
-    head_row = lax.broadcasted_iota(jnp.int32, (CH, 1), 0) // 64
-    kept = jnp.zeros((CH, 1), F32)
-    last_e = jnp.exp(rates[0, :, TOK - 1 : TOK])
-    for h in range(HEADS):
-        kept = jnp.where(head_row == h, last_e[h : h + 1, 0:1], kept)
-    fstate_ref[...] = kept * prior.astype(F32) + new_t.T
+    fstate_ref[...] = carry[...] + new_t.T
 
     for copy in sends:
         copy.wait_send()
-    if not fast:
-        flag_ref[0] = 0
 
 
 def put(*refs):
-    srcs, dsts, mids, sem = refs[0:3], refs[3:6], refs[6:9], refs[9]
-    gets = [pltpu.make_async_copy(src, mid, sem.at[k]) for k, (src, mid) in enumerate(zip(srcs, mids))]
-    puts = [pltpu.make_async_copy(mid, dst, sem.at[3 + k]) for k, (mid, dst) in enumerate(zip(mids, dsts))]
-    for get in gets:
-        get.start()
-    for get, one in zip(gets, puts):
-        get.wait()
-        one.start()
-    for one in puts:
-        one.wait()
+    srcs, dsts, sem = refs[0:3], refs[3:6], refs[6]
+    copies = [pltpu.make_async_copy(src, dst, sem.at[k]) for k, (src, dst) in enumerate(zip(srcs, dsts))]
+    for copy in copies:
+        copy.start()
+    for copy in copies:
+        copy.wait()
 
 
 def on_device(
@@ -496,73 +475,60 @@
         conv_weight, conv_bias.reshape(1, CH),
     )
 
-    def layer(fast):
-        return pl.pallas_call(
-            functools.partial(body, fast),
-            out_shape=(*shapes, jax.ShapeDtypeStruct((1,), jnp.int32)),
-            in_specs=[smem] * 6 + [hbm] * 6 + [vmem] * 2,
-            out_specs=(vmem, vmem, vmem, smem),
-            scratch_shapes=[
-                pltpu.VMEM((2, 2, 4, 4, 256, 256), BF),
-                pltpu.VMEM((Z, 512, 256), BF),
-                pltpu.VMEM((2 * HELD, 128, 256) if fast else (Z, 256, 256), BF),
-                pltpu.VMEM((Z, 16, 256), BF),
-                pltpu.VMEM((2, 4, 64, 512), BF),
-                pltpu.VMEM((2, STEPS, 128, 256), BF),
-                pltpu.VMEM((2, STEPS, 128, 256), BF),
-                pltpu.VMEM((Z, 128), jnp.int32),
-                pltpu.SMEM((Z, 128), jnp.int32),
-                pltpu.VMEM((256, 256), F32),
-                pltpu.VMEM((4, 512), BF),
-                pltpu.VMEM((3, 1, 256), F32),
-                pltpu.VMEM((512, 256), F32),
-                pltpu.VMEM((2, 16, 512), F32),
-                pltpu.VMEM((8 + TOK, 256), F32),
-                pltpu.VMEM((256, 512), BF),
-                pltpu.VMEM((512, 256), BF),
-                pltpu.VMEM((512, 512), F32),
-                pltpu.VMEM((4, 512, 512), BF),
-                pltpu.VMEM((4, 512, 256), BF),
-                pltpu.VMEM((2, 8, 512), F32),
-                pltpu.VMEM((3, 512, 128), F32),
-                dma((7,)),
-                dma((2, 8, WSUB)),
-                dma((2, 8, WSUB)),
-                dma((2, 8, SSUB)),
-                dma((2, 8, SSUB)),
-                dma((2, 8, 1)),
-                dma((2, 8, 1)),
-                dma((2, 4, 4)),
-                dma((2, 4, 4)),
-                dma((2, 4)),
-                dma((2, 4)),
-                dma((5,)),
-                dma((5,)),
-                dma((2, STEPS)),
-                dma((2, STEPS)),
-                dma,
-            ],
-            compiler_params=pltpu.CompilerParams(
-                collective_id=0 if fast else 1, has_side_effects=True, vmem_limit_bytes=56 * 1024 * 1024
-            ),
-        )(*args)
-
-    *results, left = layer(True)
-
-    def place(*values):
-        return pl.pallas_call(
-            put,
-            out_shape=shapes,
-            in_specs=[hbm] * 3,
-            out_specs=[hbm] * 3,
-            scratch_shapes=[pltpu.VMEM(v.shape, v.dtype) for v in shapes] + [dma((6,))],
-            compiler_params=pltpu.CompilerParams(vmem_limit_bytes=60 * 1024 * 1024),
-        )(*values)
-
-    def again(*_):
-        return tuple(layer(False)[0:3])
-
-    out, fstate, ftail = lax.cond(left[0] == 0, place, again, *results)
+    results = pl.pallas_call(
+        body,
+        out_shape=shapes,
+        in_specs=[smem] * 6 + [hbm] * 6 + [vmem] * 2,
+        out_specs=(vmem, vmem, vmem),
+        scratch_shapes=[
+            pltpu.VMEM((2, 2, 4, 4, 256, 256), BF),
+            pltpu.VMEM((Z, 512, 256), BF),
+            pltpu.VMEM((2 * HELD, 128, 256), BF),
+            pltpu.VMEM((Z, 16, 256), BF),
+            pltpu.VMEM((2, 4, 64, 512), BF),
+            pltpu.VMEM((2, STEPS, 128, 256), BF),
+            pltpu.VMEM((2, STEPS, 128, 256), BF),
+            pltpu.VMEM((Z, 128), jnp.int32),
+            pltpu.SMEM((Z, 128), jnp.int32),
+            pltpu.VMEM((256, 256), F32),
+            pltpu.VMEM((4, 512), BF),
+            pltpu.VMEM((3, 1, 256), F32),
+            pltpu.VMEM((512, 256), F32),
+            pltpu.VMEM((2, 16, 512), F32),
+            pltpu.VMEM((8 + TOK, 256), F32),
+            pltpu.VMEM((256, 512), BF),
+            pltpu.VMEM((512, 256), BF),
+            pltpu.VMEM((512, 512), F32),
+            pltpu.VMEM((4, 512, 512), BF),
+            pltpu.VMEM((4, 512, 256), BF),
+            pltpu.VMEM((2, 8, 512), F32),
+            pltpu.VMEM((3, 512, 128), F32),
+            pltpu.VMEM((512, 256), F32),
+            pltpu.VMEM((512, 256), F32),
+            pltpu.VMEM((256, 256), F32),
+            dma((7,)),
+            dma((2, 8, WSUB)),
+            dma((2, 8, WSUB)),
+            dma((2, 8, 1)),
+            dma((2, 8, 1)),
+            dma((2, 4, 4)),
+            dma((2, 4, 4)),
+            dma((2, 4)),
+            dma((2, 4)),
+            dma((5,)),
+            dma((5,)),
+            dma((2, STEPS)),
+            dma((2, STEPS)),
+            dma,
+        ],
+        compiler_params=pltpu.CompilerParams(
+            collective_id=0, has_side_effects=True, vmem_limit_bytes=56 * 1024 * 1024
+        ),
+    )(*args)
+
+    out, fstate, ftail = pl.pallas_call(
+        put, out_shape=shapes, in_specs=[vmem] * 3, out_specs=[hbm] * 3, scratch_shapes=[dma((3,))]
+    )(*results)
     return out, fstate.reshape(1, HEADS, 64, N), ftail.transpose(1, 0, 2)
 
 

time: 82.1 us -> 81.3 us (level)
  Pallas kernels: 76.4 us -> 79.9 us
  local copies, waits for them, and re-layouts: 3.3 us -> 0 us
  between operations: 2.14 us -> 1.29 us
    pallas_call x2, Pallas kernels: 76.4 us -> 79.9 us  [the longest x1 78 us: on_device(): pl.pallas_call(body, out_shape=shapes, in_specs=[smem] * 6 + [hbm] * 6 +...]
    unnamed x29 -> x0, local copies, waits for them, and re-layouts: 3.3 us -> none
where the time goes in v3:
time: 81.3 us; the launch traced here: 81.2 us
  Pallas kernels  79.9 us (98%)
  between operations  1.29 us (2%)
    pallas_call x1, Pallas kernels, on_device(): pl.pallas_call(body, out_shape=shapes, in_specs=[smem] * 6 + [hbm] * 6 +...  78 us
    pallas_call x1, Pallas kernels, on_device(): pl.pallas_call(put, out_shape=shapes, in_specs=[vmem] * 3, out_specs=[hbm...  1.85 us

profile of v3, /device:TPU:6, one launch (start us, length us, event | category | flops | bytes accessed | tf_op | source)
XLA Modules:
  0.0 81.2 jit_solution(1331521682724169111)
XLA Ops:
  1.3 78.0 %shard_map.157 = (bf16[512,256]{1,0:T(8,128)(2,1)}, f32[256,256]{1,0:T(8,128)}, f32[3,1,256]{2,1,0:T(1,128)}) custom-call(s32[16]{0:T(128)} %request_state.1, s32[16]{0:T(128)} %owner_map.1, s32[1]{0:T(128)S(6)} %copy.17.shared_id, f32[4]{0:T(128)} %step_bias.1, f32[4]{0:T(128)} %decay_log.1, f32[4]{0:T(128)} %skip_gain.1, bf16[512,256]{1,0:T(8,128)(2,1)} %x_hbm.1, ...), custom_call_target="tpu_custom_call" | custom-call | tf_op jit(solution)/shard_map/pallas_call | solution.py:478
  79.3 1.8 %shard_map.158 = (bf16[512,256]{1,0:T(8,128)(2,1)}, f32[256,256]{1,0:T(8,128)}, f32[3,1,256]{2,1,0:T(1,128)}) custom-call(bf16[512,256]{1,0:T(8,128)(2,1)} %get-tuple-element.9.refs_0_, f32[256,256]{1,0:T(8,128)} %get-tuple-element.10.refs_1_, f32[3,1,256]{2,1,0:T(1,128)} %get-tuple-element.11.refs_2_), custom_call_target="tpu_custom_call" | custom-call | tf_op jit(solution)/shard_map/pallas_call | solution.py:529

commit v4 on v3

--- a/solution.py
+++ b/solution.py
@@ -20,11 +20,13 @@
 
 
 def body(
-    request_state, owner_map, shared_id, step_bias, decay_log, skip_gain,
-    x_hbm, w_hbm, sw_hbm, tail_hbm, state_hbm, g_hbm, conv_w, conv_b,
+    request_hbm, owner_hbm, shared_hbm, bias_hbm, decay_hbm, gain_hbm,
+    x_hbm, w_hbm, sw_hbm, tail_hbm, state_hbm, g_hbm, cw_hbm, cb_hbm,
+    out_hbm, fstate_hbm, ftail_hbm,
     out_ref, fstate_ref, ftail_ref,
+    request_state, owner_map, shared_id, step_bias, decay_log, skip_gain, conv_w, conv_b,
     A, W, S, M, G, stage, landed, plan_v, plan, state_own, sw_own, tail_own, acc, sacc, ext, inT, outv, score, mix, xbd, rates, rate_t, base, weigh, carry,
-    loc_sem, ws_sem, wr_sem, ms_sem, mr_sem, as_sem, ar_sem, cs_sem, cr_sem, gs_sem, gr_sem, vs_sem, vr_sem, plan_sem,
+    loc_sem, out_sem, ws_sem, wr_sem, ms_sem, mr_sem, as_sem, ar_sem, cs_sem, cr_sem, gs_sem, gr_sem, vs_sem, vr_sem, plan_sem,
 ):
     z = lax.axis_index("rep")
     hid = lax.axis_index("head")
@@ -96,6 +98,14 @@
         pltpu.make_async_copy(x_hbm.at[0:256], A.at[0, c, y, x], loc_sem.at[4]),
         pltpu.make_async_copy(x_hbm.at[256:512], A.at[1, c, x, y], loc_sem.at[5]),
         pltpu.make_async_copy(g_hbm, G.at[c, y], loc_sem.at[6]),
+        pltpu.make_async_copy(request_hbm, request_state, loc_sem.at[7]),
+        pltpu.make_async_copy(owner_hbm, owner_map, loc_sem.at[8]),
+        pltpu.make_async_copy(shared_hbm, shared_id, loc_sem.at[9]),
+        pltpu.make_async_copy(bias_hbm, step_bias, loc_sem.at[10]),
+        pltpu.make_async_copy(decay_hbm, decay_log, loc_sem.at[11]),
+        pltpu.make_async_copy(gain_hbm, skip_gain, loc_sem.at[12]),
+        pltpu.make_async_copy(cw_hbm, conv_w, loc_sem.at[13]),
+        pltpu.make_async_copy(cb_hbm, conv_b, loc_sem.at[14]),
     ]
     for copy in locs:
         copy.start()
@@ -351,12 +361,14 @@
         base[...] = expand(rate_t[1])
         weigh[...] = expand(rate_t[2])
 
+    def put_tail():
+        j = (z - state_row(z) + Z) % Z
+        ext[0:8, :] = jnp.concatenate([jnp.zeros((5, CH), F32), M[j].astype(F32)[8:11]], axis=0)
+
     def resume():
         row = state_row(z)
-        j_state = (z - row + Z) % Z
         prior = jnp.concatenate([prior_half(row, 0), prior_half(row, 1)], axis=0)
         base[...] *= lax.dot_general(outv[...], prior, (((1,), (1,)), ((), ())), preferred_element_type=F32)
-        ext[0:8, :] = jnp.concatenate([jnp.zeros((5, CH), F32), M[j_state].astype(F32)[8:11]], axis=0)
         head_row = lax.broadcasted_iota(jnp.int32, (CH, 1), 0) // 64
         kept = jnp.zeros((CH, 1), F32)
         last_e = jnp.exp(rates[0, :, TOK - 1 : TOK])
@@ -369,8 +381,8 @@
     def add(u, f, *args):
         work[u].append((f, args))
 
-    for t in range(1, STEPS + 1):
-        add(2 + 30 * t // STEPS, convey, t)
+    for t in range(1, STEPS):
+        add(2 + 33 * t // STEPS, convey, t)
     for s, u in enumerate((0, 4, 6, 8, 10, 13, 15, 18, 20)):
         if s:
             add(u, m_step, s)
@@ -397,16 +409,18 @@
     add(24, decays)
     for h in range(HEADS):
         add(25 + h, make_mix, h)
+    add(27, put_tail)
     add(28, expand_decays)
     add(28, project, 0)
     add(29, projects, 1, 3)
     add(30, projects, 3, 5)
     add(31, projects, 5, 7)
     add(32, projects, 7, 8)
-    add(32, resume)
 
     m_step(0)
     both(a_one, 0)
+    for i in range(7, 15):
+        locs[i].wait()
     make_plan()
     convey(0)
     w_step(0, (2, 3))
@@ -417,11 +431,19 @@
         for f, args in work[u]:
             f(*args)
 
+    leaving = []
+
+    def leave(src, dst, k):
+        copy = pltpu.make_async_copy(src, dst, out_sem.at[k])
+        copy.start()
+        leaving.append(copy)
+
     project(8)
     projected = acc[...].astype(BF).astype(F32)
     ext[8 : 8 + TOK, :] = projected
     for k in range(3):
         ftail_ref[k] = ext[TOK + 5 + k : TOK + 6 + k, :]
+    leave(ftail_ref, ftail_hbm, 0)
     conv = conv_b[...] + conv_w[0:1, :] * ext[5 : 5 + TOK, :]
     for k in range(1, 4):
         conv = conv + conv_w[k : k + 1, :] * ext[5 + k : 5 + k + TOK, :]
@@ -431,20 +453,27 @@
     for h in range(HEADS):
         skip = jnp.where(one == h, skip_gain[h], skip)
         xbd[h] = jnp.where(chan == h, conv_f, 0.0).astype(BF)
-    rest = base[...] + skip * conv_f
     for tb in range(2):
         rows = pl.ds(256 * tb, 256)
         cols = 256 * (tb + 1)
-        inner = rest[256 * tb : 256 * tb + 256]
+        inner = (skip * conv_f)[256 * tb : 256 * tb + 256]
         for h in range(HEADS):
             inner = inner + jnp.dot(mix[h, rows, 0:cols], xbd[h, 0:cols, :], preferred_element_type=F32)
-        out_ref[rows, :] = inner.astype(BF)
+        acc[rows, :] = inner
     weighted = (conv_f * weigh[...]).astype(BF)
     new_t = jnp.dot(inT[...], weighted, preferred_element_type=F32)
+    convey(STEPS)
+    resume()
     fstate_ref[...] = carry[...] + new_t.T
-
+    leave(fstate_ref, fstate_hbm, 1)
+    for tb in range(2):
+        rows = pl.ds(256 * tb, 256)
+        out_ref[rows, :] = (acc[rows, :] + base[rows, :]).astype(BF)
+        leave(out_ref.at[rows], out_hbm.at[rows], 2 + tb)
     for copy in sends:
         copy.wait_send()
+    for copy in leaving:
+        copy.wait()
 
 
 def put(*refs):
@@ -478,9 +507,18 @@
     results = pl.pallas_call(
         body,
         out_shape=shapes,
-        in_specs=[smem] * 6 + [hbm] * 6 + [vmem] * 2,
-        out_specs=(vmem, vmem, vmem),
+        in_specs=[hbm] * 14,
+        out_specs=(hbm, hbm, hbm),
         scratch_shapes=[
+            *[pltpu.VMEM(v.shape, v.dtype) for v in shapes],
+            pltpu.SMEM((16,), jnp.int32),
+            pltpu.SMEM((16,), jnp.int32),
+            pltpu.SMEM((1,), jnp.int32),
+            pltpu.SMEM((4,), F32),
+            pltpu.SMEM((4,), F32),
+            pltpu.SMEM((4,), F32),
+            pltpu.VMEM((4, 256), F32),
+            pltpu.VMEM((1, 256), F32),
             pltpu.VMEM((2, 2, 4, 4, 256, 256), BF),
             pltpu.VMEM((Z, 512, 256), BF),
             pltpu.VMEM((2 * HELD, 128, 256), BF),
@@ -506,7 +544,8 @@
             pltpu.VMEM((512, 256), F32),
             pltpu.VMEM((512, 256), F32),
             pltpu.VMEM((256, 256), F32),
-            dma((7,)),
+            dma((15,)),
+            dma((4,)),
             dma((2, 8, WSUB)),
             dma((2, 8, WSUB)),
             dma((2, 8, 1)),

time: 81.3 us -> 79.7 us (0.980)
  Pallas kernels: 79.9 us -> 78.2 us
    pallas_call x1, Pallas kernels: 78 us -> 76.4 us  [on_device(): pl.pallas_call(body, out_shape=shapes, in_specs=[hbm] * 14, out_specs=(hb...]
where the time goes in v4:
time: 79.7 us; the launch traced here: 79.5 us
  Pallas kernels  78.2 us (98%)
  between operations  1.29 us (2%)
    pallas_call x1, Pallas kernels, on_device(): pl.pallas_call(body, out_shape=shapes, in_specs=[hbm] * 14, out_specs=(hb...  76.4 us
    pallas_call x1, Pallas kernels, on_device(): pl.pallas_call(put, out_shape=shapes, in_specs=[vmem] * 3, out_specs=[hbm...  1.85 us

profile of v4, /device:TPU:6, one launch (start us, length us, event | category | flops | bytes accessed | tf_op | source)
XLA Modules:
  0.0 79.5 jit_solution(8362754036943388733)
XLA Ops:
  1.3 76.4 %shard_map.157 = (bf16[512,256]{1,0:T(8,128)(2,1)}, f32[256,256]{1,0:T(8,128)}, f32[3,1,256]{2,1,0:T(1,128)}) custom-call(s32[16]{0:T(128)} %request_hbm.1, s32[16]{0:T(128)} %owner_hbm.1, s32[1]{0:T(128)S(6)} %copy.17.shared_hbm, f32[4]{0:T(128)} %bias_hbm.1, f32[4]{0:T(128)} %decay_hbm.1, f32[4]{0:T(128)} %gain_hbm.1, bf16[512,256]{1,0:T(8,128)(2,1)} %x_hbm.1, ...), custom_call_target="tpu_custom_call" | custom-call | tf_op jit(solution)/shard_map/pallas_call | solution.py:507
  77.7 1.8 %shard_map.158 = (bf16[512,256]{1,0:T(8,128)(2,1)}, f32[256,256]{1,0:T(8,128)}, f32[3,1,256]{2,1,0:T(1,128)}) custom-call(bf16[512,256]{1,0:T(8,128)(2,1)} %get-tuple-element.9.refs_0_, f32[256,256]{1,0:T(8,128)} %get-tuple-element.10.refs_1_, f32[3,1,256]{2,1,0:T(1,128)} %get-tuple-element.11.refs_2_), custom_call_target="tpu_custom_call" | custom-call | tf_op jit(solution)/shard_map/pallas_call | solution.py:568

commit v5 on v4

--- a/solution.py
+++ b/solution.py
@@ -565,6 +565,7 @@
         ),
     )(*args)
 
+    results = lax.cond(shared_id[0] >= 0, lambda *v: v, lambda *v: tuple(jnp.zeros_like(u) for u in v), *results)
     out, fstate, ftail = pl.pallas_call(
         put, out_shape=shapes, in_specs=[vmem] * 3, out_specs=[hbm] * 3, scratch_shapes=[dma((3,))]
     )(*results)

time: 79.7 us -> 78.7 us (0.987)
  Pallas kernels: 78.2 us -> 77.2 us
    pallas_call x1, Pallas kernels: 1.85 us -> 0.82 us  [on_device(): pl.pallas_call(put, out_shape=shapes, in_specs=[vmem] * 3, out_specs=[hbm...]
where the time goes in v5:
time: 78.7 us; the launch traced here: 78.6 us
  Pallas kernels  77.2 us (98%)
  between operations  1.3 us (2%)
    pallas_call x1, Pallas kernels, on_device(): pl.pallas_call(body, out_shape=shapes, in_specs=[hbm] * 14, out_specs=(hb...  76.4 us

profile of v5, /device:TPU:6, one launch (start us, length us, event | category | flops | bytes accessed | tf_op | source)
XLA Modules:
  0.0 78.6 jit_solution(4571556732786452856)
XLA Ops:
  1.3 76.4 %shard_map.157 = (bf16[512,256]{1,0:T(8,128)(2,1)S(1)}, f32[256,256]{1,0:T(8,128)S(1)}, f32[3,1,256]{2,1,0:T(1,128)S(1)}) custom-call(s32[16]{0:T(128)} %request_hbm.1, s32[16]{0:T(128)} %owner_hbm.1, s32[1]{0:T(128)S(6)} %copy.23.shared_hbm, f32[4]{0:T(128)} %bias_hbm.1, f32[4]{0:T(128)} %decay_hbm.1, f32[4]{0:T(128)} %gain_hbm.1, bf16[512,256]{1,0:T(8,128)(2,1)} %x_hbm.1, ...), custom_call_target="tpu_custom_call" | custom-call | tf_op jit(solution)/shard_map/pallas_call | solution.py:507
  77.7 0.8 %shard_map.158 = (bf16[512,256]{1,0:T(8,128)(2,1)}, f32[256,256]{1,0:T(8,128)}, f32[3,1,256]{2,1,0:T(1,128)}) custom-call(bf16[512,256]{1,0:T(8,128)(2,1)S(1)} %get-tuple-element.15.refs_0_, f32[256,256]{1,0:T(8,128)S(1)} %get-tuple-element.16.refs_1_, f32[3,1,256]{2,1,0:T(1,128)S(1)} %get-tuple-element.17.refs_2_), custom_call_target="tpu_custom_call" | custom-call | tf_op jit(solution)/shard_map/pallas_call | solution.py:569
  (1 shorter events, 0.0 us)

commit v6 on v5

--- a/solution.py
+++ b/solution.py
@@ -22,11 +22,10 @@
 def body(
     request_hbm, owner_hbm, shared_hbm, bias_hbm, decay_hbm, gain_hbm,
     x_hbm, w_hbm, sw_hbm, tail_hbm, state_hbm, g_hbm, cw_hbm, cb_hbm,
-    out_hbm, fstate_hbm, ftail_hbm,
     out_ref, fstate_ref, ftail_ref,
     request_state, owner_map, shared_id, step_bias, decay_log, skip_gain, conv_w, conv_b,
     A, W, S, M, G, stage, landed, plan_v, plan, state_own, sw_own, tail_own, acc, sacc, ext, inT, outv, score, mix, xbd, rates, rate_t, base, weigh, carry,
-    loc_sem, out_sem, ws_sem, wr_sem, ms_sem, mr_sem, as_sem, ar_sem, cs_sem, cr_sem, gs_sem, gr_sem, vs_sem, vr_sem, plan_sem,
+    loc_sem, ws_sem, wr_sem, ms_sem, mr_sem, as_sem, ar_sem, cs_sem, cr_sem, gs_sem, gr_sem, vs_sem, vr_sem, plan_sem,
 ):
     z = lax.axis_index("rep")
     hid = lax.axis_index("head")
@@ -431,19 +430,11 @@
         for f, args in work[u]:
             f(*args)
 
-    leaving = []
-
-    def leave(src, dst, k):
-        copy = pltpu.make_async_copy(src, dst, out_sem.at[k])
-        copy.start()
-        leaving.append(copy)
-
     project(8)
     projected = acc[...].astype(BF).astype(F32)
     ext[8 : 8 + TOK, :] = projected
     for k in range(3):
         ftail_ref[k] = ext[TOK + 5 + k : TOK + 6 + k, :]
-    leave(ftail_ref, ftail_hbm, 0)
     conv = conv_b[...] + conv_w[0:1, :] * ext[5 : 5 + TOK, :]
     for k in range(1, 4):
         conv = conv + conv_w[k : k + 1, :] * ext[5 + k : 5 + k + TOK, :]
@@ -465,15 +456,11 @@
     convey(STEPS)
     resume()
     fstate_ref[...] = carry[...] + new_t.T
-    leave(fstate_ref, fstate_hbm, 1)
     for tb in range(2):
         rows = pl.ds(256 * tb, 256)
         out_ref[rows, :] = (acc[rows, :] + base[rows, :]).astype(BF)
-        leave(out_ref.at[rows], out_hbm.at[rows], 2 + tb)
     for copy in sends:
         copy.wait_send()
-    for copy in leaving:
-        copy.wait()
 
 
 def put(*refs):
@@ -508,9 +495,8 @@
         body,
         out_shape=shapes,
         in_specs=[hbm] * 14,
-        out_specs=(hbm, hbm, hbm),
+        out_specs=(vmem, vmem, vmem),
         scratch_shapes=[
-            *[pltpu.VMEM(v.shape, v.dtype) for v in shapes],
             pltpu.SMEM((16,), jnp.int32),
             pltpu.SMEM((16,), jnp.int32),
             pltpu.SMEM((1,), jnp.int32),
@@ -545,7 +531,6 @@
             pltpu.VMEM((512, 256), F32),
             pltpu.VMEM((256, 256), F32),
             dma((15,)),
-            dma((4,)),
             dma((2, 8, WSUB)),
             dma((2, 8, WSUB)),
             dma((2, 8, 1)),

time: 78.7 us -> 78.2 us (level)
  no operation moved by 1% of the time
where the time goes in v6:
time: 78.2 us; the launch traced here: 78 us
  Pallas kernels  76.7 us (98%)
  between operations  1.3 us (2%)
    pallas_call x1, Pallas kernels, on_device(): pl.pallas_call(body, out_shape=shapes, in_specs=[hbm] * 14, out_specs=(vm...  75.9 us

profile of v6, /device:TPU:6, one launch (start us, length us, event | category | flops | bytes accessed | tf_op | source)
XLA Modules:
  0.0 78.0 jit_solution(15754040833773574803)
XLA Ops:
  1.3 75.9 %shard_map.157 = (bf16[512,256]{1,0:T(8,128)(2,1)S(1)}, f32[256,256]{1,0:T(8,128)S(1)}, f32[3,1,256]{2,1,0:T(1,128)S(1)}) custom-call(s32[16]{0:T(128)} %request_hbm.1, s32[16]{0:T(128)} %owner_hbm.1, s32[1]{0:T(128)S(6)} %copy.23.shared_hbm, f32[4]{0:T(128)} %bias_hbm.1, f32[4]{0:T(128)} %decay_hbm.1, f32[4]{0:T(128)} %gain_hbm.1, bf16[512,256]{1,0:T(8,128)(2,1)} %x_hbm.1, ...), custom_call_target="tpu_custom_call" | custom-call | tf_op jit(solution)/shard_map/pallas_call | solution.py:494
  77.2 0.8 %shard_map.158 = (bf16[512,256]{1,0:T(8,128)(2,1)}, f32[256,256]{1,0:T(8,128)}, f32[3,1,256]{2,1,0:T(1,128)}) custom-call(bf16[512,256]{1,0:T(8,128)(2,1)S(1)} %get-tuple-element.15.refs_0_, f32[256,256]{1,0:T(8,128)S(1)} %get-tuple-element.16.refs_1_, f32[3,1,256]{2,1,0:T(1,128)S(1)} %get-tuple-element.17.refs_2_), custom_call_target="tpu_custom_call" | custom-call | tf_op jit(solution)/shard_map/pallas_call | solution.py:554
  (1 shorter events, 0.0 us)

commit v7 on v6

--- a/solution.py
+++ b/solution.py
@@ -381,7 +381,7 @@
         work[u].append((f, args))
 
     for t in range(1, STEPS):
-        add(2 + 33 * t // STEPS, convey, t)
+        add(2 + 31 * t // STEPS, convey, t)
     for s, u in enumerate((0, 4, 6, 8, 10, 13, 15, 18, 20)):
         if s:
             add(u, m_step, s)
@@ -426,7 +426,7 @@
     g_ring(0)
     for u in range(3, 36):
         if u > 3:
-            w_step(u // 4, (u % 4,))
+            w_step(u // 4, ((0, 2, 1, 3)[u % 4],))
         for f, args in work[u]:
             f(*args)
 

time: 78.2 us -> 78.8 us (level)
  no operation moved by 1% of the time
where the time goes in v7:
time: 78.8 us; the launch traced here: 78.7 us
  Pallas kernels  77.4 us (98%)
  between operations  1.3 us (2%)
    pallas_call x1, Pallas kernels, on_device(): pl.pallas_call(body, out_shape=shapes, in_specs=[hbm] * 14, out_specs=(vm...  76.5 us

profile of v7, /device:TPU:6, one launch (start us, length us, event | category | flops | bytes accessed | tf_op | source)
XLA Modules:
  0.0 78.7 jit_solution(5362485321907998206)
XLA Ops:
  1.3 76.5 %shard_map.157 = (bf16[512,256]{1,0:T(8,128)(2,1)S(1)}, f32[256,256]{1,0:T(8,128)S(1)}, f32[3,1,256]{2,1,0:T(1,128)S(1)}) custom-call(s32[16]{0:T(128)} %request_hbm.1, s32[16]{0:T(128)} %owner_hbm.1, s32[1]{0:T(128)S(6)} %copy.23.shared_hbm, f32[4]{0:T(128)} %bias_hbm.1, f32[4]{0:T(128)} %decay_hbm.1, f32[4]{0:T(128)} %gain_hbm.1, bf16[512,256]{1,0:T(8,128)(2,1)} %x_hbm.1, ...), custom_call_target="tpu_custom_call" | custom-call | tf_op jit(solution)/shard_map/pallas_call | solution.py:494
  77.9 0.8 %shard_map.158 = (bf16[512,256]{1,0:T(8,128)(2,1)}, f32[256,256]{1,0:T(8,128)}, f32[3,1,256]{2,1,0:T(1,128)}) custom-call(bf16[512,256]{1,0:T(8,128)(2,1)S(1)} %get-tuple-element.15.refs_0_, f32[256,256]{1,0:T(8,128)S(1)} %get-tuple-element.16.refs_1_, f32[3,1,256]{2,1,0:T(1,128)S(1)} %get-tuple-element.17.refs_2_), custom_call_target="tpu_custom_call" | custom-call | tf_op jit(solution)/shard_map/pallas_call | solution.py:554
  (1 shorter events, 0.0 us)
